TPU v7x, 128 devices: a whole 4x4x4 slice. The times are simulated.
128 devices in a mesh: ctx: 32 (over z, x, core), user: 4 (over y).
Axes of the slice: x: 4, y: 4, z: 4, core: 2. Of those that a mesh axis runs over, the one named last changes fastest.
Arguments:
- robe_array: bfloat16 [524288, 128], P(('ctx', 'user')), may hold values from -6 to 6
- block_owner: int32 [4, 32768, 4], P('user', 'ctx'), may hold values from 0 to 127, all different within a row; in each aligned block of 1024 rows (0 to 1023, 1024 to 2047, ..., all dimensions but the last counted through in order) at most 80 rows name the same one
- block_slot: int32 [4, 32768, 4], P('user', 'ctx'), may hold values from 0 to 4095
- w_query: bfloat16 [512, 512], replicated, may hold values from -0.25 to 0.25
- w_key: bfloat16 [512, 512], replicated, may hold values from -0.25 to 0.25
- w_value: bfloat16 [512, 512], replicated, may hold values from -0.25 to 0.25
- w_gate: bfloat16 [512, 512], replicated, may hold values from -0.25 to 0.25
- w_output: bfloat16 [512, 512], replicated, may hold values from -0.25 to 0.25
- head_gain: float32 [512], replicated, may hold values from 0.1 to 1.9
Outputs:
- encoded: bfloat16 [4, 32768, 512], P('user', 'ctx')
Inputs may be any that keep to these rules, and one draw needn't show every extreme that they name: `block_owner`: the four owners of one position differ; over the positions of one device no owner is named more than 80 times, a bound that some block reaches.
All inputs are finite; a program needn't handle non-finite values.
Results may differ from a plain program's by a relative error of at most 0.015.
Values may be sent and summed in bfloat16 or wider, within the bound.
A program may use at most 128 MiB of HBM per device.

v0:
```python
import math

import jax
import jax.numpy as jnp
from jax import lax
from jax.sharding import PartitionSpec as P

HEADS = 4


def entering(value, axis, join, neutral):
    count, mine = (lax.axis_size(axis), lax.axis_index(axis))
    pieces = lax.all_gather(value, axis)
    total = jnp.full_like(value, 0) + jnp.asarray(neutral, value.dtype)

    def hop(position, total):
        longer = join(total, pieces[position])
        return jnp.where(position < mine, longer, total)

    return lax.fori_loop(0, count - 1, hop, total)


def table_lookup(index_flat, table):
    total_rows = index_flat.shape[0]
    table_rows = table.shape[0]
    step = math.gcd(total_rows, 512)
    index_blocks = index_flat.reshape(total_rows // step, step)
    columns = jnp.arange(table_rows, dtype=jnp.int32)

    def fetch_block(index_rows):
        picker = (index_rows[:, None] == columns[None, :]).astype(jnp.bfloat16)
        return jnp.dot(picker, table, preferred_element_type=jnp.float32).astype(jnp.bfloat16)

    found = lax.map(fetch_block, index_blocks)
    return found.reshape(total_rows, table.shape[1])


def shards(
    robe_array, block_owner, block_slot, w_query, w_key, w_value, w_gate, w_output, head_gain
):
    ctx_size = lax.axis_size("ctx")
    user_size = lax.axis_size("user")
    devices = ctx_size * user_size
    positions = block_owner.shape[1]
    parts = block_owner.shape[2]
    block_width = robe_array.shape[1]
    capacity = max(10 * positions // devices, 2)
    owners = block_owner.reshape(-1)
    slots = block_slot.reshape(-1)
    total_rows = owners.shape[0]
    owner_hot = (owners[:, None] == jnp.arange(devices, dtype=jnp.int32)[None, :]).astype(
        jnp.bfloat16
    )
    step = min(512, total_rows)
    nblocks = total_rows // step
    hot_blocks = owner_hot.reshape(nblocks, step, devices)
    lower = jnp.tril(jnp.ones((step, step), jnp.bfloat16))
    inside = jnp.einsum("ts,bsd->btd", lower, hot_blocks, preferred_element_type=jnp.float32)
    block_totals = jnp.sum(hot_blocks.astype(jnp.float32), axis=1)
    before = jnp.cumsum(block_totals, axis=0) - block_totals
    counts = (inside + before[:, None, :]).reshape(total_rows, devices)
    slot_rank = (jnp.sum(counts * owner_hot.astype(jnp.float32), axis=1) - 1.0).astype(jnp.int32)
    rank_hot = (slot_rank[:, None] == jnp.arange(capacity, dtype=jnp.int32)[None, :]).astype(
        jnp.float32
    )
    weighted = rank_hot * slots.astype(jnp.float32)[:, None]
    requests = jnp.einsum(
        "rd,rc->dc", owner_hot.astype(jnp.float32), weighted, precision=lax.Precision.HIGHEST
    ).astype(jnp.int32)
    arrived = lax.all_to_all(requests, ("ctx", "user"), split_axis=0, concat_axis=0, tiled=True)
    fetched = table_lookup(arrived.reshape(-1), robe_array).reshape(devices, capacity, block_width)
    returned = lax.all_to_all(fetched, ("ctx", "user"), split_axis=0, concat_axis=0, tiled=True)
    flat_returned = returned.reshape(devices * capacity, block_width)
    flat_index = owners * capacity + slot_rank
    embed = table_lookup(flat_index, flat_returned).reshape(positions, parts * block_width)
    queries = jnp.dot(embed, w_query, preferred_element_type=jnp.float32).astype(jnp.bfloat16)
    keys_in = jnp.dot(embed, w_key, preferred_element_type=jnp.float32).astype(jnp.bfloat16)
    values_in = jnp.dot(embed, w_value, preferred_element_type=jnp.float32).astype(jnp.bfloat16)
    gates = jnp.dot(embed, w_gate, preferred_element_type=jnp.float32).astype(jnp.bfloat16)
    width = embed.shape[1]
    head_size = width // HEADS
    block_rows = min(512, positions)
    count = positions // block_rows
    qblocks = (jax.nn.elu(queries.astype(jnp.float32)) + 1.0).reshape(
        count, block_rows, HEADS, head_size
    )
    kblocks = (jax.nn.elu(keys_in.astype(jnp.float32)) + 1.0).reshape(
        count, block_rows, HEADS, head_size
    )
    vblocks = values_in.astype(jnp.float32).reshape(count, block_rows, HEADS, head_size)
    causal = jnp.tril(jnp.ones((block_rows, block_rows), jnp.float32))
    scores = (
        jnp.einsum("bthe,bshe->bhts", qblocks, kblocks, precision=lax.Precision.HIGHEST)
        * causal[None, None]
    )
    local = jnp.einsum("bhts,bshe->bthe", scores, vblocks, precision=lax.Precision.HIGHEST)
    block_states = jnp.einsum("bshe,bshf->bhef", kblocks, vblocks, precision=lax.Precision.HIGHEST)
    total = jnp.sum(block_states, axis=0)
    empty = jnp.zeros_like(total)
    earlier = entering(total, "ctx", lambda first, second: first + second, empty)
    within = jnp.cumsum(block_states, axis=0) - block_states + earlier[None]
    carried = jnp.einsum("bthe,bhef->bthf", qblocks, within, precision=lax.Precision.HIGHEST)
    mixed = (local + carried).reshape(positions, HEADS, head_size)
    mean_square = jnp.mean(mixed * mixed, axis=-1, keepdims=True)
    normed = mixed / jnp.sqrt(mean_square + 1e-06) * head_gain.reshape(HEADS, head_size)[None]
    gated = (normed.reshape(positions, width) * jax.nn.silu(gates.astype(jnp.float32))).astype(
        jnp.bfloat16
    )
    encoded = jnp.dot(gated, w_output, preferred_element_type=jnp.float32).astype(jnp.bfloat16)
    return encoded.reshape(1, positions, width)


def solution(mesh):
    return jax.shard_map(
        shards,
        mesh=mesh,
        in_specs=(
            P(("ctx", "user"), None),
            P("user", "ctx", None),
            P("user", "ctx", None),
            P(),
            P(),
            P(),
            P(),
            P(),
            P(),
        ),
        out_specs=P("user", "ctx", None),
        check_vma=False,
    )
```

profile of v0, /device:TPU:1, one launch (start us, length us, event | category | flops | bytes accessed | tf_op | source)
XLA Modules:
  0.0 280.7 jit_solution(9275626218727596999)
XLA Ops:
  9.9 3.5 %fusion.43 = s32[128,1,80]{0,2,1:T(8,128)S(1)} fusion(f32[4096]{0:T(1024)S(1)} %convert_element_type.77, s32[4096]{0:T(1024)S(1)} %bitcast.86, s32[4096]{0:T(1024)S(1)} %eq.70), kind=kOutput, calls=%fused_computation.62 | convolution fusion | flops 504506368 | bytes 90112 | tf_op jit(solution)/shard_map/rd,rc->dc/dot_general | solution.py:67
  14.2 11.5 %all-to-all-start = ((s32[128,1,80]{2,1,0:T(1,128)}), s32[128,1,80]{2,1,0:T(1,128)S(1)}, u32[]{:S(2)}, u32[]{:S(2)}) async-start(s32[128,1,80]{2,1,0:T(1,128)} %copy.42), calls=%async_computation | async-start | bytes 131072 | tf_op jit(solution)/shard_map/all_to_all | solution.py:70
  25.7 9.6 %all-to-all-done = s32[128,1,80]{2,1,0:T(1,128)S(1)} async-done(((s32[128,1,80]{2,1,0:T(1,128)}), s32[128,1,80]{2,1,0:T(1,128)S(1)}, u32[]{:S(2)}, u32[]{:S(2)}) %all-to-all-start) | async-done | bytes 40992 | tf_op jit(solution)/shard_map/all_to_all | solution.py:70
  36.7 43.8 %while.36 = (s32[]{:T(128)}, bf16[20,512,128]{2,1,0:T(8,128)(2,1)}, s32[20,512]{1,0:T(8,128)S(1)}, bf16[4096,128]{1,0:T(8,128)(2,1)S(1)}, s32[]{:T(128)}) while((s32[]{:T(128)}, bf16[20,512,128]{2,1,0:T(8,128)(2,1)}, s32[20,512]{1,0:T(8,128)S(1)}, bf16[4096,128]{1,0:T(8,128)(2,1)S(1)}, s32[]{:T(128)}) %tuple.79), condition=%wide.region_4.5_spmd.clone, body=%wide.region_3.4_spmd.clone.sunk | while | flops 539033600 | bytes 1186369 | solution.py:34
  36.7 2.2 fusion.85
  38.9 2.2 fusion.85
  41.1 2.2 fusion.85
  43.3 2.2 fusion.85
  45.5 2.2 fusion.85
  47.7 2.2 fusion.85
  49.9 2.2 fusion.85
  52.0 2.2 fusion.85
  54.2 2.2 fusion.85
  56.4 2.2 fusion.85
  58.6 2.2 fusion.85
  60.8 2.2 fusion.85
  63.0 2.2 fusion.85
  65.2 2.2 fusion.85
  67.4 2.2 fusion.85
  69.6 2.2 fusion.85
  71.8 2.2 fusion.85
  74.0 2.2 fusion.85
  76.1 2.2 fusion.85
  78.3 2.2 fusion.85
  80.5 4.2 %all-to-all-start.1 = ((bf16[128,80,128]{2,1,0:T(8,128)(2,1)}), bf16[128,80,128]{2,1,0:T(8,128)(2,1)S(1)}, u32[]{:S(2)}, u32[]{:S(2)}) async-start(bf16[128,80,128]{2,1,0:T(8,128)(2,1)} %bitcast.79), calls=%async_computation.1 | async-start | bytes 5242880 | tf_op jit(solution)/shard_map/all_to_all | solution.py:72
  85.0 36.0 %all-to-all-done.1 = bf16[128,80,128]{2,1,0:T(8,128)(2,1)S(1)} async-done(((bf16[128,80,128]{2,1,0:T(8,128)(2,1)}), bf16[128,80,128]{2,1,0:T(8,128)(2,1)S(1)}, u32[]{:S(2)}, u32[]{:S(2)}) %all-to-all-start.1) | async-done | bytes 2621472 | tf_op jit(solution)/shard_map/all_to_all | solution.py:72
  121.0 33.6 %while.37 = (s32[]{:T(128)}, bf16[8,512,128]{2,1,0:T(8,128)(2,1)}, s32[8,512]{1,0:T(8,128)S(1)}, bf16[10240,128]{1,0:T(8,128)(2,1)S(1)}, s32[]{:T(128)}) while((s32[]{:T(128)}, bf16[8,512,128]{2,1,0:T(8,128)(2,1)}, s32[8,512]{1,0:T(8,128)S(1)}, bf16[10240,128]{1,0:T(8,128)(2,1)S(1)}, s32[]{:T(128)}) %tuple.77), condition=%wide.region_6.7_spmd.clone, body=%wide.region_5.6_spmd.clone.sunk | while | flops 1347485696 | bytes 2759233 | solution.py:34
  121.0 4.2 %fusion.87 = bf16[8,512,128]{2,1,0:T(8,128)(2,1)} fusion(bf16[8,512,128]{2,1,0:T(8,128)(2,1)} %get-tuple-element.300, s32[]{:T(128)} %get-tuple-element.299, bf16[10240,128]{1,0:T(8,128)(2,1)S(1)} %get-tuple-element.307, s32[512]{0:T(512)S(1)} %bitcast.85), kind=kOutput, calls=%fused_computation.14.clone.1 | convolution fusion | flops 1347485696 | bytes 2755072 | tf_op jit(solution)/shard_map/while/body/eval_jaxpr/dot_general | solution.py:32
  125.2 4.2 %fusion.87 = bf16[8,512,128]{2,1,0:T(8,128)(2,1)} fusion(bf16[8,512,128]{2,1,0:T(8,128)(2,1)} %get-tuple-element.300, s32[]{:T(128)} %get-tuple-element.299, bf16[10240,128]{1,0:T(8,128)(2,1)S(1)} %get-tuple-element.307, s32[512]{0:T(512)S(1)} %bitcast.85), kind=kOutput, calls=%fused_computation.14.clone.1 | convolution fusion | flops 1347485696 | bytes 2755072 | tf_op jit(solution)/shard_map/while/body/eval_jaxpr/dot_general | solution.py:32
  129.4 4.2 %fusion.87 = bf16[8,512,128]{2,1,0:T(8,128)(2,1)} fusion(bf16[8,512,128]{2,1,0:T(8,128)(2,1)} %get-tuple-element.300, s32[]{:T(128)} %get-tuple-element.299, bf16[10240,128]{1,0:T(8,128)(2,1)S(1)} %get-tuple-element.307, s32[512]{0:T(512)S(1)} %bitcast.85), kind=kOutput, calls=%fused_computation.14.clone.1 | convolution fusion | flops 1347485696 | bytes 2755072 | tf_op jit(solution)/shard_map/while/body/eval_jaxpr/dot_general | solution.py:32
  133.6 4.2 %fusion.87 = bf16[8,512,128]{2,1,0:T(8,128)(2,1)} fusion(bf16[8,512,128]{2,1,0:T(8,128)(2,1)} %get-tuple-element.300, s32[]{:T(128)} %get-tuple-element.299, bf16[10240,128]{1,0:T(8,128)(2,1)S(1)} %get-tuple-element.307, s32[512]{0:T(512)S(1)} %bitcast.85), kind=kOutput, calls=%fused_computation.14.clone.1 | convolution fusion | flops 1347485696 | bytes 2755072 | tf_op jit(solution)/shard_map/while/body/eval_jaxpr/dot_general | solution.py:32
  137.8 4.2 %fusion.87 = bf16[8,512,128]{2,1,0:T(8,128)(2,1)} fusion(bf16[8,512,128]{2,1,0:T(8,128)(2,1)} %get-tuple-element.300, s32[]{:T(128)} %get-tuple-element.299, bf16[10240,128]{1,0:T(8,128)(2,1)S(1)} %get-tuple-element.307, s32[512]{0:T(512)S(1)} %bitcast.85), kind=kOutput, calls=%fused_computation.14.clone.1 | convolution fusion | flops 1347485696 | bytes 2755072 | tf_op jit(solution)/shard_map/while/body/eval_jaxpr/dot_general | solution.py:32
  142.0 4.2 %fusion.87 = bf16[8,512,128]{2,1,0:T(8,128)(2,1)} fusion(bf16[8,512,128]{2,1,0:T(8,128)(2,1)} %get-tuple-element.300, s32[]{:T(128)} %get-tuple-element.299, bf16[10240,128]{1,0:T(8,128)(2,1)S(1)} %get-tuple-element.307, s32[512]{0:T(512)S(1)} %bitcast.85), kind=kOutput, calls=%fused_computation.14.clone.1 | convolution fusion | flops 1347485696 | bytes 2755072 | tf_op jit(solution)/shard_map/while/body/eval_jaxpr/dot_general | solution.py:32
  146.2 4.2 %fusion.87 = bf16[8,512,128]{2,1,0:T(8,128)(2,1)} fusion(bf16[8,512,128]{2,1,0:T(8,128)(2,1)} %get-tuple-element.300, s32[]{:T(128)} %get-tuple-element.299, bf16[10240,128]{1,0:T(8,128)(2,1)S(1)} %get-tuple-element.307, s32[512]{0:T(512)S(1)} %bitcast.85), kind=kOutput, calls=%fused_computation.14.clone.1 | convolution fusion | flops 1347485696 | bytes 2755072 | tf_op jit(solution)/shard_map/while/body/eval_jaxpr/dot_general | solution.py:32
  150.4 4.2 %fusion.87 = bf16[8,512,128]{2,1,0:T(8,128)(2,1)} fusion(bf16[8,512,128]{2,1,0:T(8,128)(2,1)} %get-tuple-element.300, s32[]{:T(128)} %get-tuple-element.299, bf16[10240,128]{1,0:T(8,128)(2,1)S(1)} %get-tuple-element.307, s32[512]{0:T(512)S(1)} %bitcast.85), kind=kOutput, calls=%fused_computation.14.clone.1 | convolution fusion | flops 1347485696 | bytes 2755072 | tf_op jit(solution)/shard_map/while/body/eval_jaxpr/dot_general | solution.py:32
  154.6 2.5 reshape_reshape.11
  157.1 2.5 fusion.25
  159.6 1.8 reshape.124
  161.4 2.0 copy.46
  163.4 3.7 %convolution_convert_fusion.4 = bf16[1024,512]{1,0:T(8,128)(2,1)} fusion(bf16[1024,512]{1,0:T(8,128)(2,1)} %reshape_reshape.11, bf16[512,512]{1,0:T(8,128)(2,1)S(1)} %copy-done.6), kind=kOutput, calls=%fused_computation.57 | convolution fusion | flops 537395200 | bytes 2621440 | tf_op jit(solution)/shard_map/dot_general | solution.py:78
  167.0 2.1 reshape.122
  169.2 3.1 %fusion.64 = (f32[4,128,128]{2,1,0:T(8,128)}, f32[2,4,128,128]{3,2,1,0:T(8,128)S(1)}) fusion(f32[2,512,4,128]{1,3,2,0:T(8,128)S(1)} %copy.46, bf16[2,512,4,128]{3,2,1,0:T(4,128)(2,1)} %reshape.122), kind=kOutput, calls=%fused_computation.84 | convolution fusion | flops 805371904 | bytes 3932160 | tf_op jit(solution)/shard_map/bshe,bshf->bhef/dot_general | solution.py:97
  172.4 1.1 fusion.50
  173.4 4.1 %fusion.23 = f32[1024,512]{1,0:T(8,128)} fusion(bf16[1024,512]{1,0:T(8,128)(2,1)} %reshape_reshape.11, bf16[512,512]{1,0:T(8,128)(2,1)} %param.18), kind=kOutput, calls=%fused_computation.34 | convolution fusion | flops 540016640 | bytes 3670016 | tf_op jit(solution)/shard_map/dot_general | solution.py:76
  177.5 2.0 reshape.123
  179.5 10.3 %fusion.34 = f32[2,4,512,512]{3,2,1,0:T(8,128)} fusion(f32[2,512,4,128]{1,3,2,0:T(8,128)} %copy-done.1, f32[2,512,4,128]{3,2,1,0:T(4,128)S(1)} %reshape.123), kind=kOutput, calls=%fused_computation.51 | convolution fusion | flops 3221225472 | bytes 12582912 | tf_op jit(solution)/shard_map/bthe,bshe->bhts/dot_general | solution.py:93
  189.8 31.7 %all-gather.3.cloned.1.call-done = f32[128,128,128]{2,1,0:T(8,128)} async-done(((f32[4,128,128]{2,1,0:T(8,128)}), f32[128,128,128]{2,1,0:T(8,128)}) %all-gather.3.cloned.1.call-update) | async-done | bytes 8388624 | tf_op jit(solution)/shard_map/all_gather | solution.py:13
  221.5 33.0 %while.38 = (s32[]{:T(128)}, f32[4,128,128]{2,1,0:T(8,128)S(1)}, s32[]{:T(128)}, f32[32,4,128,128]{3,2,1,0:T(8,128)}, s32[]{:T(128)}, /*index=5*/s32[]{:T(128)}) while((s32[]{:T(128)}, f32[4,128,128]{2,1,0:T(8,128)S(1)}, s32[]{:T(128)}, f32[32,4,128,128]{3,2,1,0:T(8,128)}, s32[]{:T(128)}, /*index=5*/s32[]{:T(128)}) %tuple.78), condition=%wide.region_10.11_spmd.clone, body=%wide.region_9.10_spmd.clone.sunk | while | flops 196612 | bytes 786525 | solution.py:20
  222.6 1.0 add_select_fusion.2
  223.7 1.0 add_select_fusion.2
  224.7 1.0 add_select_fusion.2
  229.0 1.0 add_select_fusion.2
  230.0 1.0 add_select_fusion.2
  235.4 1.0 add_select_fusion.2
  236.4 1.0 add_select_fusion.2
  241.8 1.0 add_select_fusion.2
  242.8 1.0 add_select_fusion.2
  249.2 1.0 add_select_fusion.2
  250.3 1.0 add_select_fusion.2
  254.7 2.0 fusion.32
  256.8 8.9 %multiply_reduce_fusion = (f32[2,512,4]{1,2,0:T(4,128)S(1)}, f32[2,512,4,128]{1,3,2,0:T(8,128)S(1)}) fusion(f32[2,4,128,512]{3,2,1,0:T(8,128)S(1)} %fusion.32, f32[2,4,512,512]{3,2,1,0:T(8,128)} %fusion.34, f32[512,512]{1,0:T(8,128)S(1)} %copy-done.2, bf16[2,512,4,128]{3,2,1,0:T(4,128)(2,1)S(1)} %copy-done.3), kind=kOutput, calls=%fused_computation.39 | convolution fusion | flops 3224891392 | bytes 14696448 | tf_op jit(solution)/shard_map/bhts,bshe->bthe/dot_general | solution.py:96
  265.9 1.9 copy.50
  267.8 1.2 div.23
  269.0 4.8 %fusion.38 = bf16[1,1024,512]{2,1,0:T(8,128)(2,1)} fusion(bf16[512,512]{1,0:T(8,128)(2,1)} %param.22, f32[128,8,4,128]{3,2,1,0:T(4,128)S(1)} %bitcast.80, f32[128,8,4,128]{3,2,1,0:T(4,128)} %bitcast.81, bf16[1024,512]{1,0:T(8,128)(2,1)} %reshape_reshape.11, bf16[512,512]{1,0:T(8,128)(2,1)} %param.21, f32[512]{0:T(512)S(1)} %copy-done.7), kind=kOutput, calls=%fused_computation.58 | convolution fusion | flops 1079508992 | bytes 7342080 | tf_op jit(solution)/shard_map/dot_general | solution.py:109
  (89 shorter events, 27.1 us)
Async XLA Ops:
  6.5 150.5 %copy-start = (bf16[512,512]{1,0:T(8,128)(2,1)S(1)}, bf16[512,512]{1,0:T(8,128)(2,1)}, u32[]{:S(2)}) copy-start(bf16[512,512]{1,0:T(8,128)(2,1)} %param.19) | copy-start | bytes 1572868
  8.4 1.0 copy-start.4
  9.4 27.3 %copy-start.5 = (bf16[4096,128]{1,0:T(8,128)(2,1)S(1)}, bf16[4096,128]{1,0:T(8,128)(2,1)}, u32[]{:S(2)}) copy-start(bf16[4096,128]{1,0:T(8,128)(2,1)} %param.15) | copy-start | bytes 3145732
  14.2 21.1 %all-to-all-start = ((s32[128,1,80]{2,1,0:T(1,128)}), s32[128,1,80]{2,1,0:T(1,128)S(1)}, u32[]{:S(2)}, u32[]{:S(2)}) async-start(s32[128,1,80]{2,1,0:T(1,128)} %copy.42), calls=%async_computation | async-start | bytes 131072 | tf_op jit(solution)/shard_map/all_to_all | solution.py:70
  80.5 40.5 %all-to-all-start.1 = ((bf16[128,80,128]{2,1,0:T(8,128)(2,1)}), bf16[128,80,128]{2,1,0:T(8,128)(2,1)S(1)}, u32[]{:S(2)}, u32[]{:S(2)}) async-start(bf16[128,80,128]{2,1,0:T(8,128)(2,1)} %bitcast.79), calls=%async_computation.1 | async-start | bytes 5242880 | tf_op jit(solution)/shard_map/all_to_all | solution.py:72
  84.7 136.8 %all-gather.3.cloned.1.call-start = ((), (), s32[]{:S(2)}) async-start(), calls=%async_computation.2 | async-start | bytes 8650752 | tf_op jit(solution)/shard_map/all_gather | solution.py:13
  161.4 2.0 copy-start.6
  163.4 5.8 %copy-start.1 = (f32[2,512,4,128]{1,3,2,0:T(8,128)}, f32[2,512,4,128]{1,3,2,0:T(8,128)S(1)}, u32[]{:S(2)}) copy-start(f32[2,512,4,128]{1,3,2,0:T(8,128)S(1)} %copy.46) | copy-start | bytes 6291460
  254.7 2.1 copy-start.2
  254.7 2.1 copy-start.3
  267.8 1.2 copy-start.7
Sparse Core Ops, SparseCore 0:
  172.5 49.0 all-gather.2
where the time goes:
time: 282 us; the launch traced here: 281 us
  matrix products  121 us (43%)
  waiting for transfers between devices  77.3 us (27%)
  other arithmetic  34.6 us (12%)
  local copies, waits for them, and re-layouts  17.3 us (6%)
  starting transfers between devices  15.9 us (6%)
  between operations  13.7 us (5%)
    dot_general x28, matrix products, fetch_block(): jnp.dot(picker, table, preferred_element_type=jnp.float32)  77.2 us
    all_to_all x1, waiting for transfers between devices, shards(): lax.all_to_all(fetched, ('ctx', 'user'), split_axis=0, concat_axis=0, til...  36 us
    select_n x31, other arithmetic, hop(): return jnp.where(position < mine, longer, total)  32.3 us
    all_gather x1, waiting for transfers between devices, entering(): pieces = lax.all_gather(value, axis)  31.7 us
    all_to_all x1, starting transfers between devices, shards(): lax.all_to_all(requests, ('ctx', 'user'), split_axis=0, concat_axis=0, ti...  11.5 us
    dot_general x1, matrix products, shards(): jnp.einsum('bthe,bshe->bhts', qblocks, kblocks, precision=lax.Precision.H...  10.3 us
    all_to_all x1, waiting for transfers between devices, shards(): lax.all_to_all(requests, ('ctx', 'user'), split_axis=0, concat_axis=0, ti...  9.55 us
    dot_general x1, matrix products, shards(): jnp.einsum('bhts,bshe->bthe', scores, vblocks, precision=lax.Precision.HI...  8.88 us
  transfers between devices with their start and end apart: 3, of which 3 were waited for; matrix products, arithmetic and copies ran while one was open for 6% of the time, Pallas kernels for 0%

commit v1 on v0

v1 whole, which is shorter than its diff:
```python
import jax
import jax.numpy as jnp
from jax import lax
from jax.experimental import pallas as pl
from jax.experimental.pallas import tpu as pltpu
from jax.sharding import PartitionSpec as P

MESH = pl.DeviceIdType.MESH
HEADS = 4
HEAD = 128
CAP = 80
GROUP = 16
CHUNK = 256
F32 = jnp.float32
BF16 = jnp.bfloat16


def moved(k, sign):
    c, y = lax.axis_index("ctx"), lax.axis_index("user")
    core, r = k % 2, k // 2
    a, b, e = r % 4, (r // 4) % 4, r // 16
    z = (c // 8 + 8 + sign * (a + b + e)) % 4
    x = ((c // 2) % 4 + 8 + sign * a) % 4
    u = (y + 8 + sign * (a + b)) % 4
    return z * 8 + x * 2 + (c + core) % 2, u


def rank_kernel(own_ref, slot_ref, req, index_ref):
    devices = req.shape[0]
    parts, positions = own_ref.shape
    device_row = lax.broadcasted_iota(jnp.int32, (devices, CHUNK), 0)
    rank_row = lax.broadcasted_iota(jnp.int32, (128, CHUNK), 0)
    upper = (
        lax.broadcasted_iota(jnp.int32, (CHUNK, CHUNK), 0)
        <= lax.broadcasted_iota(jnp.int32, (CHUNK, CHUNK), 1)
    ).astype(F32).astype(BF16)
    before = jnp.zeros((devices, 1), F32)
    total = jnp.zeros((devices, 256), F32)
    for j in range(parts):
        for p in range(0, positions, CHUNK):
            own = own_ref[j : j + 1, p : p + CHUNK]
            slot = slot_ref[j : j + 1, p : p + CHUNK]
            named = device_row == own
            hot = jnp.where(named, 1.0, 0.0).astype(BF16)
            count = jnp.dot(hot, upper, preferred_element_type=F32) + before
            before = count[:, CHUNK - 1 :]
            rank = jnp.sum(jnp.where(named, count, 0.0), axis=0, keepdims=True).astype(jnp.int32) - 1
            index_ref[j : j + 1, p : p + CHUNK] = own * CAP + rank
            at_rank = rank_row == rank
            high = jnp.where(at_rank, (slot // 64).astype(F32), 0.0).astype(BF16)
            low = jnp.where(at_rank, (slot % 64).astype(F32), 0.0).astype(BF16)
            total += lax.dot_general(
                hot, jnp.concatenate([high, low], axis=0), (((1,), (1,)), ((), ())),
                preferred_element_type=F32,
            )
    req[...] = (total[:, :128] * 64.0 + total[:, 128:]).astype(jnp.int32)


def rank(owner, slot):
    devices = lax.axis_size("ctx") * lax.axis_size("user")
    vmem = pl.BlockSpec(memory_space=pltpu.VMEM)
    return pl.pallas_call(
        rank_kernel,
        out_shape=(
            jax.ShapeDtypeStruct((devices, 128), jnp.int32),
            jax.ShapeDtypeStruct(owner.shape, jnp.int32),
        ),
        in_specs=[vmem] * 2,
        out_specs=(vmem, vmem),
        name="rank",
    )(owner, slot)


def fetch_kernel(
    req, table_ref, rows_ref,
    landed, arrived, table, gathered, send, recv,
    req_out, req_in, own_sem, row_out, row_in,
):
    devices = send.shape[0]
    groups = devices // GROUP
    me = lax.axis_index("ctx") * lax.axis_size("user") + lax.axis_index("user")
    barrier = pltpu.get_barrier_semaphore()

    def greet(k, carry):
        pl.semaphore_signal(barrier, inc=1, device_id=moved(k, 1), device_id_type=MESH)
        return carry

    lax.fori_loop(1, devices, greet, 0)

    def widen(k, carry):
        s = pl.ds(pl.multiple_of(k * 256, 256), 256)
        table[s] = table_ref[s].astype(F32)
        return carry

    lax.fori_loop(0, table.shape[0] // 256, widen, 0)

    pl.semaphore_wait(barrier, devices - 1)

    def ask(k, carry):
        ctx, user = moved(k, 1)
        owner = ctx * lax.axis_size("user") + user
        pltpu.make_async_remote_copy(
            req.at[pl.ds(owner, 1)], landed.at[pl.ds(me, 1)], req_out, req_in.at[k // GROUP],
            device_id=(ctx, user), device_id_type=MESH,
        ).start()
        return carry

    lax.fori_loop(1, devices, ask, 0)
    landed[pl.ds(me, 1)] = req[pl.ds(me, 1)]
    for g in range(groups):
        some = req.at[pl.ds(0, GROUP - (1 if g == 0 else 0))]
        pltpu.make_async_copy(some, some, req_in.at[g]).wait()
    mine = pltpu.make_async_copy(landed, arrived, own_sem)
    mine.start()
    mine.wait()

    def gather(asker):
        for i in range(CAP):
            gathered[pl.ds(i, 1)] = table[pl.ds(arrived[asker, i], 1)]
        return gathered[...].astype(BF16)

    def answer(k, carry):
        ctx, user = moved(k, -1)
        asker = ctx * lax.axis_size("user") + user
        send[asker] = gather(asker)
        pltpu.make_async_remote_copy(
            send.at[asker], recv.at[me], row_out, row_in.at[k // GROUP],
            device_id=(ctx, user), device_id_type=MESH,
        ).start()
        return carry

    for g in range(groups):
        first = 1 if g == 0 else 0
        lax.fori_loop(g * GROUP + first, (g + 1) * GROUP, answer, 0)
    recv[me] = gather(me)

    def unpack(k, carry):
        ctx, user = moved(k, 1)
        owner = ctx * lax.axis_size("user") + user
        rows_ref[owner] = recv[owner].astype(F32)
        return carry

    for g in range(groups):
        first = 1 if g == 0 else 0
        some = recv.at[pl.ds(0, GROUP - first)]
        pltpu.make_async_copy(some, some, row_in.at[g]).wait()
        lax.fori_loop(g * GROUP, (g + 1) * GROUP, unpack, 0)
    some = req.at[pl.ds(0, devices - 1)]
    pltpu.make_async_copy(some, some, req_out).wait()
    some = send.at[pl.ds(0, devices - 1)]
    pltpu.make_async_copy(some, some, row_out).wait()


def fetch(requests, table):
    devices = lax.axis_size("ctx") * lax.axis_size("user")
    vmem = pl.BlockSpec(memory_space=pltpu.VMEM)
    return pl.pallas_call(
        fetch_kernel,
        out_shape=jax.ShapeDtypeStruct((devices, CAP, table.shape[1]), F32),
        in_specs=[vmem] * 2,
        out_specs=vmem,
        scratch_shapes=[
            pltpu.VMEM((devices, 128), jnp.int32),
            pltpu.SMEM((devices, 128), jnp.int32),
            pltpu.VMEM(table.shape, F32),
            pltpu.VMEM((CAP, table.shape[1]), F32),
            pltpu.VMEM((devices, CAP, table.shape[1]), BF16),
            pltpu.VMEM((devices, CAP, table.shape[1]), BF16),
            pltpu.SemaphoreType.DMA,
            pltpu.SemaphoreType.DMA((devices // GROUP,)),
            pltpu.SemaphoreType.DMA,
            pltpu.SemaphoreType.DMA,
            pltpu.SemaphoreType.DMA((devices // GROUP,)),
        ],
        compiler_params=pltpu.CompilerParams(
            collective_id=0, has_side_effects=True, vmem_limit_bytes=48 << 20
        ),
        name="fetch",
    )(requests, table)


def attend_kernel(
    index_ref, rows_ref, wq_ref, wk_ref, wv_ref, wg_ref, wo_ref, gain_ref, out_ref,
    embed, fq, fk, values, gates, intra, state, packed, from_each, earlier, entering,
    out_a, in_a, out_b, in_b,
):
    ctx_size = lax.axis_size("ctx")
    ctx, user = lax.axis_index("ctx"), lax.axis_index("user")
    barrier = pltpu.get_barrier_semaphore()

    def greet(k, carry):
        pl.semaphore_signal(
            barrier, inc=1, device_id=((ctx + k) % ctx_size, user), device_id_type=MESH
        )
        return carry

    lax.fori_loop(1, ctx_size, greet, 0)

    parts, positions = index_ref.shape
    chunks = positions // CHUNK

    def collect(b, carry):
        for i in range(16):
            for j in range(parts):
                embed[j, pl.ds(b * 16 + i, 1)] = rows_ref[pl.ds(index_ref[j, b * 16 + i], 1)]
        return carry

    lax.fori_loop(0, positions // 16, collect, 0)

    def feature(v):
        v = v.astype(BF16).astype(F32)
        return jnp.where(v > 0, v + 1.0, jnp.exp(jnp.minimum(v, 0.0))).astype(BF16)

    running = [jnp.zeros((HEAD, HEAD), F32)] * HEADS
    for c in range(chunks):
        at = pl.ds(c * CHUNK, CHUNK)
        e = jnp.concatenate([embed[j, at] for j in range(parts)], axis=1).astype(BF16)
        k = feature(jnp.dot(e, wk_ref[...], preferred_element_type=F32))
        v = jnp.dot(e, wv_ref[...], preferred_element_type=F32).astype(BF16)
        fk[at] = k
        values[at] = v
        for h in range(HEADS):
            s = slice(h * HEAD, (h + 1) * HEAD)
            state[c, h] = running[h]
            running[h] = running[h] + lax.dot_general(
                k[:, s], v[:, s], (((0,), (0,)), ((), ())), preferred_element_type=F32
            )
    rows = HEADS * HEAD // ctx_size
    for h in range(HEADS):
        for i in range(HEAD // rows):
            packed[h * (HEAD // rows) + i] = running[h][i * rows : (i + 1) * rows].astype(BF16)

    pl.semaphore_wait(barrier, ctx_size - 1)

    def part_out(k, carry):
        other = (ctx + k) % ctx_size
        pltpu.make_async_remote_copy(
            packed.at[other], from_each.at[ctx], out_a, in_a,
            device_id=(other, user), device_id_type=MESH,
        ).start()
        return carry

    lax.fori_loop(1, ctx_size, part_out, 0)
    from_each[ctx] = packed[ctx]

    causal = lax.broadcasted_iota(jnp.int32, (CHUNK, CHUNK), 0) >= lax.broadcasted_iota(
        jnp.int32, (CHUNK, CHUNK), 1
    )

    def local(c):
        at = pl.ds(c * CHUNK, CHUNK)
        e = jnp.concatenate([embed[j, at] for j in range(parts)], axis=1).astype(BF16)
        q = feature(jnp.dot(e, wq_ref[...], preferred_element_type=F32))
        fq[at] = q
        gates[at] = jnp.dot(e, wg_ref[...], preferred_element_type=F32).astype(BF16)
        for h in range(HEADS):
            s = slice(h * HEAD, (h + 1) * HEAD)
            scores = lax.dot_general(
                q[:, s], fk[at, s], (((1,), (1,)), ((), ())), preferred_element_type=F32
            )
            scores = jnp.where(causal, scores, 0.0).astype(BF16)
            intra[at, s] = jnp.dot(scores, values[at, s], preferred_element_type=F32)

    for c in range(chunks // 2):
        local(c)

    some = packed.at[pl.ds(0, ctx_size - 1)]
    pltpu.make_async_copy(some, some, in_a).wait()
    pltpu.make_async_copy(some, some, out_a).wait()
    sofar = jnp.zeros((rows, HEAD), F32)
    for i in range(ctx_size):
        earlier[i] = sofar.astype(BF16)
        sofar = sofar + from_each[i].astype(F32)

    def part_back(k, carry):
        other = (ctx + k) % ctx_size
        pltpu.make_async_remote_copy(
            earlier.at[other], entering.at[ctx], out_b, in_b,
            device_id=(other, user), device_id_type=MESH,
        ).start()
        return carry

    lax.fori_loop(1, ctx_size, part_back, 0)
    entering[ctx] = earlier[ctx]

    for c in range(chunks // 2, chunks):
        local(c)

    pltpu.make_async_copy(some, some, in_b).wait()
    pltpu.make_async_copy(some, some, out_b).wait()

    for c in range(chunks):
        at = pl.ds(c * CHUNK, CHUNK)
        heads = []
        for h in range(HEADS):
            s = slice(h * HEAD, (h + 1) * HEAD)
            n = HEAD // rows
            came = entering[h * n : (h + 1) * n].reshape(HEAD, HEAD).astype(F32)
            within = (state[c, h] + came).astype(BF16)
            mixed = intra[at, s] + jnp.dot(fq[at, s], within, preferred_element_type=F32)
            square = jnp.mean(mixed * mixed, axis=1, keepdims=True)
            gate = gates[at, s].astype(F32)
            normed = mixed * lax.rsqrt(square + 1e-6) * gain_ref[:, s]
            heads.append((normed * (gate / (1.0 + jnp.exp(-gate)))).astype(BF16))
        out_ref[at] = jnp.dot(
            jnp.concatenate(heads, axis=1), wo_ref[...], preferred_element_type=F32
        ).astype(BF16)


def attend(index, rows, wq, wk, wv, wg, wo, gain):
    ctx_size = lax.axis_size("ctx")
    parts, positions = index.shape
    width = wq.shape[1]
    vmem = pl.BlockSpec(memory_space=pltpu.VMEM)
    piece = pltpu.VMEM((ctx_size, HEADS * HEAD // ctx_size, HEAD), BF16)
    return pl.pallas_call(
        attend_kernel,
        out_shape=jax.ShapeDtypeStruct((positions, width), BF16),
        in_specs=[pl.BlockSpec(memory_space=pltpu.SMEM)] + [vmem] * 7,
        out_specs=vmem,
        scratch_shapes=[
            pltpu.VMEM((parts, positions, width // parts), F32),
            pltpu.VMEM((positions, width), BF16),
            pltpu.VMEM((positions, width), BF16),
            pltpu.VMEM((positions, width), BF16),
            pltpu.VMEM((positions, width), BF16),
            pltpu.VMEM((positions, width), F32),
            pltpu.VMEM((positions // CHUNK, HEADS, HEAD, HEAD), F32),
            piece, piece, piece, piece,
            pltpu.SemaphoreType.DMA,
            pltpu.SemaphoreType.DMA,
            pltpu.SemaphoreType.DMA,
            pltpu.SemaphoreType.DMA,
        ],
        compiler_params=pltpu.CompilerParams(
            collective_id=1, has_side_effects=True, vmem_limit_bytes=48 << 20
        ),
        name="attend",
    )(index, rows, wq, wk, wv, wg, wo, gain)


def shards(
    robe_array, block_owner, block_slot, w_query, w_key, w_value, w_gate, w_output, head_gain
):
    owner = jnp.swapaxes(block_owner[0], 0, 1)
    slot = jnp.swapaxes(block_slot[0], 0, 1)
    requests, index = rank(owner, slot)
    rows = fetch(requests, robe_array)
    encoded = attend(
        index, rows.reshape(-1, rows.shape[2]), w_query, w_key, w_value, w_gate, w_output,
        head_gain.reshape(1, -1),
    )
    return encoded[None]


def solution(mesh):
    return jax.shard_map(
        shards,
        mesh=mesh,
        in_specs=(
            P(("ctx", "user"), None),
            P("user", "ctx", None),
            P("user", "ctx", None),
            P(),
            P(),
            P(),
            P(),
            P(),
            P(),
        ),
        out_specs=P("user", "ctx", None),
        check_vma=False,
    )
```

time: 282 us -> 92.9 us (0.33)
  matrix products: 121 us -> 0 us
  Pallas kernels: 0 us -> 89.4 us
  waiting for transfers between devices: 77.3 us -> 0 us
  other arithmetic: 34.6 us -> 0 us
  starting transfers between devices: 15.9 us -> 0 us
  local copies, waits for them, and re-layouts: 17.3 us -> 3.07 us
  between operations: 13.7 us -> 0.1 us
    dot_general x38 -> x0, matrix products: 121 us -> none  [the longest x28 77.2 us: fetch_block(): jnp.dot(picker, table, preferred_element_type=jnp.float32)]
    pallas_call x0 -> x3, Pallas kernels: none -> 89.4 us  [the longest x1 62.9 us: fetch(): pl.pallas_call(fetch_kernel, out_shape=jax.ShapeDtypeStruct((devices, CAP...]
    all_to_all x2 -> x0, waiting for transfers between devices: 45.6 us -> none  [the longest x1 36 us: shards(): lax.all_to_all(fetched, ('ctx', 'user'), split_axis=0, concat_axis=0, til...]
    select_n x32 -> x0, other arithmetic: 33.3 us -> none  [the longest x31 32.3 us: hop(): return jnp.where(position < mine, longer, total)]
    all_gather x1 -> x0, waiting for transfers between devices: 31.7 us -> none  [entering(): pieces = lax.all_gather(value, axis)]
    all_to_all x2 -> x0, starting transfers between devices: 15.7 us -> none  [the longest x1 11.5 us: shards(): lax.all_to_all(requests, ('ctx', 'user'), split_axis=0, concat_axis=0, ti...]
    reshape x5 -> x0, local copies, waits for them, and re-layouts: 8.16 us -> none  [the longest x2 3.76 us: shards(): (jax.nn.elu(keys_in.astype(jnp.float32)) + 1.0).reshape(count, block_rows...]
  transfers between devices with their start and end apart: 3 -> 0, of which waited for: 3 -> 0; matrix products, arithmetic and copies ran while one was open for 6% -> 0% of each run, Pallas kernels for 0% -> 0%
where the time goes in v1:
time: 92.9 us; the launch traced here: 92.6 us
  Pallas kernels  89.4 us (96%)
  local copies, waits for them, and re-layouts  3.07 us (3%)
    pallas_call x1, Pallas kernels, fetch(): pl.pallas_call(fetch_kernel, out_shape=jax.ShapeDtypeStruct((devices, CAP...  62.9 us
    pallas_call x1, Pallas kernels, attend(): pl.pallas_call(attend_kernel, out_shape=jax.ShapeDtypeStruct((positions,...  23 us
    pallas_call x1, Pallas kernels, rank(): pl.pallas_call(rank_kernel, out_shape=(jax.ShapeDtypeStruct((devices, 128...  3.54 us
    unnamed x19, local copies, waits for them, and re-layouts  3.07 us

profile of v1, /device:TPU:1, one launch (start us, length us, event | category | flops | bytes accessed | tf_op | source)
XLA Modules:
  0.0 92.6 jit_solution(1679882621262734092)
XLA Ops:
  0.0 0.0 copy-start.8
  0.0 3.5 %rank.1 = (s32[128,128]{1,0:T(8,128)}, s32[4,1024]{1,0:T(4,128)}) custom-call(s32[4,1024]{1,0:T(4,128)} %bitcast.12, s32[4,1024]{1,0:T(4,128)} %bitcast.13), custom_call_target="tpu_custom_call" | custom-call | tf_op jit(solution)/shard_map/rank/pallas_call | solution.py:62
  3.5 0.0 copy-start
  3.5 1.2 %copy-done = bf16[4096,128]{1,0:T(8,128)(2,1)S(1)} copy-done((bf16[4096,128]{1,0:T(8,128)(2,1)S(1)}, bf16[4096,128]{1,0:T(8,128)(2,1)}, u32[]{:S(2)}) %copy-start) | copy-done | bytes 1048600
  4.8 0.0 copy-start.6
  4.8 0.8 copy-done.6
  5.6 0.0 copy-start.1
  5.6 0.0 copy-start.2
  5.6 0.0 copy-start.3
  5.6 0.0 copy-start.4
  5.6 0.0 copy-start.5
  5.6 0.0 copy-start.7
  5.6 62.9 %fetch.1 = f32[128,80,128]{2,1,0:T(8,128)} custom-call(s32[128,128]{1,0:T(8,128)S(1)} %copy-done.6, bf16[4096,128]{1,0:T(8,128)(2,1)S(1)} %copy-done), custom_call_target="tpu_custom_call" | custom-call | tf_op jit(solution)/shard_map/fetch/pallas_call | solution.py:157
  68.6 0.0 copy-done.8
  68.6 0.0 copy-done.1
  68.6 0.0 copy-done.2
  68.6 0.0 copy-done.3
  68.6 0.0 copy-done.4
  68.6 0.0 copy-done.5
  68.6 0.0 copy-done.7
  68.6 23.0 %attend.1 = bf16[1024,512]{1,0:T(8,128)(2,1)S(1)} custom-call(s32[4,1024]{1,0:T(4,128)S(1)} %copy-done.7, f32[10240,128]{1,0:T(8,128)} %bitcast.11, bf16[512,512]{1,0:T(8,128)(2,1)S(1)} %copy-done.1, bf16[512,512]{1,0:T(8,128)(2,1)S(1)} %copy-done.2, bf16[512,512]{1,0:T(8,128)(2,1)S(1)} %copy-done.3, bf16[512,512]{1,0:T(8,128)(2,1)S(1)} %copy-done.4, ...), custom_call_target="tpu_custom_call" | custom-call | tf_op jit(solution)/shard_map/attend/pallas_call | solution.py:316
  91.6 1.0 %copy.11 = bf16[1,1024,512]{2,1,0:T(8,128)(2,1)} copy(bf16[1,1024,512]{2,1,0:T(8,128)(2,1)S(1)} %bitcast.9) | data formatting | bytes 2097152
Async XLA Ops:
  0.0 68.6 %copy-start.8 = (f32[512]{0:T(512)S(1)}, f32[512]{0:T(512)}, u32[]{:S(2)}) copy-start(f32[512]{0:T(512)} %param.17) | copy-start | bytes 6148
  3.5 1.2 %copy-start = (bf16[4096,128]{1,0:T(8,128)(2,1)S(1)}, bf16[4096,128]{1,0:T(8,128)(2,1)}, u32[]{:S(2)}) copy-start(bf16[4096,128]{1,0:T(8,128)(2,1)} %table_ref.1) | copy-start | bytes 3145732
  4.8 0.8 copy-start.6
  5.6 63.0 %copy-start.1 = (bf16[512,512]{1,0:T(8,128)(2,1)S(1)}, bf16[512,512]{1,0:T(8,128)(2,1)}, u32[]{:S(2)}) copy-start(bf16[512,512]{1,0:T(8,128)(2,1)} %wq_ref.1) | copy-start | bytes 1572868
  5.6 63.0 %copy-start.2 = (bf16[512,512]{1,0:T(8,128)(2,1)S(1)}, bf16[512,512]{1,0:T(8,128)(2,1)}, u32[]{:S(2)}) copy-start(bf16[512,512]{1,0:T(8,128)(2,1)} %wk_ref.1) | copy-start | bytes 1572868
  5.6 63.0 %copy-start.3 = (bf16[512,512]{1,0:T(8,128)(2,1)S(1)}, bf16[512,512]{1,0:T(8,128)(2,1)}, u32[]{:S(2)}) copy-start(bf16[512,512]{1,0:T(8,128)(2,1)} %wv_ref.1) | copy-start | bytes 1572868
  5.6 63.0 %copy-start.4 = (bf16[512,512]{1,0:T(8,128)(2,1)S(1)}, bf16[512,512]{1,0:T(8,128)(2,1)}, u32[]{:S(2)}) copy-start(bf16[512,512]{1,0:T(8,128)(2,1)} %wg_ref.1) | copy-start | bytes 1572868
  5.6 63.0 %copy-start.5 = (bf16[512,512]{1,0:T(8,128)(2,1)S(1)}, bf16[512,512]{1,0:T(8,128)(2,1)}, u32[]{:S(2)}) copy-start(bf16[512,512]{1,0:T(8,128)(2,1)} %wo_ref.1) | copy-start | bytes 1572868
  5.6 63.0 %copy-start.7 = (s32[4,1024]{1,0:T(4,128)S(1)}, s32[4,1024]{1,0:T(4,128)}, u32[]{:S(2)}) copy-start(s32[4,1024]{1,0:T(4,128)} %get-tuple-element.7.index_ref) | copy-start | bytes 49156

commit v2 on v1

--- a/solution.py
+++ b/solution.py
@@ -25,19 +25,39 @@
     return z * 8 + x * 2 + (c + core) % 2, u
 
 
-def rank_kernel(own_ref, slot_ref, req, index_ref):
-    devices = req.shape[0]
+def fetch_kernel(
+    own_ref, slot_ref, table_hbm, rows_ref, index_ref,
+    req, landed, arrived, packed, table, gathered, send, recv,
+    table_in, req_out, req_in, read_in, row_out, row_in,
+):
+    devices = send.shape[0]
+    groups = devices // GROUP
+    users = lax.axis_size("user")
+    me = lax.axis_index("ctx") * users + lax.axis_index("user")
+    barrier = pltpu.get_barrier_semaphore()
+
+    load = pltpu.make_async_copy(table_hbm, packed, table_in)
+    load.start()
+
     parts, positions = own_ref.shape
     device_row = lax.broadcasted_iota(jnp.int32, (devices, CHUNK), 0)
     rank_row = lax.broadcasted_iota(jnp.int32, (128, CHUNK), 0)
-    upper = (
+    upper = jnp.where(
         lax.broadcasted_iota(jnp.int32, (CHUNK, CHUNK), 0)
-        <= lax.broadcasted_iota(jnp.int32, (CHUNK, CHUNK), 1)
-    ).astype(F32).astype(BF16)
+        <= lax.broadcasted_iota(jnp.int32, (CHUNK, CHUNK), 1),
+        1.0, 0.0,
+    ).astype(BF16)
     before = jnp.zeros((devices, 1), F32)
+    greeted, greetings = 0, devices * CHUNK // (parts * positions)
     total = jnp.zeros((devices, 256), F32)
     for j in range(parts):
         for p in range(0, positions, CHUNK):
+            for k in range(greeted, greeted + greetings):
+                if k > 0:
+                    pl.semaphore_signal(
+                        barrier, inc=1, device_id=moved(k, 1), device_id_type=MESH
+                    )
+            greeted += greetings
             own = own_ref[j : j + 1, p : p + CHUNK]
             slot = slot_ref[j : j + 1, p : p + CHUNK]
             named = device_row == own
@@ -47,102 +67,77 @@
             rank = jnp.sum(jnp.where(named, count, 0.0), axis=0, keepdims=True).astype(jnp.int32) - 1
             index_ref[j : j + 1, p : p + CHUNK] = own * CAP + rank
             at_rank = rank_row == rank
-            high = jnp.where(at_rank, (slot // 64).astype(F32), 0.0).astype(BF16)
-            low = jnp.where(at_rank, (slot % 64).astype(F32), 0.0).astype(BF16)
+            high = jnp.where(at_rank, (slot >> 6).astype(F32), 0.0).astype(BF16)
+            low = jnp.where(at_rank, (slot & 63).astype(F32), 0.0).astype(BF16)
             total += lax.dot_general(
                 hot, jnp.concatenate([high, low], axis=0), (((1,), (1,)), ((), ())),
                 preferred_element_type=F32,
             )
-    req[...] = (total[:, :128] * 64.0 + total[:, 128:]).astype(jnp.int32)
-
-
-def rank(owner, slot):
-    devices = lax.axis_size("ctx") * lax.axis_size("user")
-    vmem = pl.BlockSpec(memory_space=pltpu.VMEM)
-    return pl.pallas_call(
-        rank_kernel,
-        out_shape=(
-            jax.ShapeDtypeStruct((devices, 128), jnp.int32),
-            jax.ShapeDtypeStruct(owner.shape, jnp.int32),
-        ),
-        in_specs=[vmem] * 2,
-        out_specs=(vmem, vmem),
-        name="rank",
-    )(owner, slot)
-
-
-def fetch_kernel(
-    req, table_ref, rows_ref,
-    landed, arrived, table, gathered, send, recv,
-    req_out, req_in, own_sem, row_out, row_in,
-):
-    devices = send.shape[0]
-    groups = devices // GROUP
-    me = lax.axis_index("ctx") * lax.axis_size("user") + lax.axis_index("user")
-    barrier = pltpu.get_barrier_semaphore()
-
-    def greet(k, carry):
-        pl.semaphore_signal(barrier, inc=1, device_id=moved(k, 1), device_id_type=MESH)
-        return carry
-
-    lax.fori_loop(1, devices, greet, 0)
+    asked = (total[:, :128] * 64.0 + total[:, 128:]).astype(jnp.int32)
+    req[...] = jnp.minimum(jnp.maximum(asked, 0), table.shape[0] - 1)
+    landed[pl.ds(0, 1)] = req[pl.ds(me, 1)]
+    load.wait()
 
     def widen(k, carry):
         s = pl.ds(pl.multiple_of(k * 256, 256), 256)
-        table[s] = table_ref[s].astype(F32)
+        table[s] = packed[s].astype(F32)
         return carry
 
     lax.fori_loop(0, table.shape[0] // 256, widen, 0)
-
     pl.semaphore_wait(barrier, devices - 1)
 
     def ask(k, carry):
         ctx, user = moved(k, 1)
-        owner = ctx * lax.axis_size("user") + user
         pltpu.make_async_remote_copy(
-            req.at[pl.ds(owner, 1)], landed.at[pl.ds(me, 1)], req_out, req_in.at[k // GROUP],
+            req.at[pl.ds(ctx * users + user, 1)], landed.at[pl.ds(k, 1)], req_out,
+            req_in.at[k // GROUP], device_id=(ctx, user), device_id_type=MESH,
+        ).start()
+        return carry
+
+    def gather(k):
+        for i in range(CAP):
+            gathered[pl.ds(i, 1)] = table[pl.ds(arrived[k, i], 1)]
+        return gathered[...].astype(BF16)
+
+    def answer(k, carry):
+        ctx, user = moved(k, -1)
+        send[k] = gather(k)
+        pltpu.make_async_remote_copy(
+            send.at[k], recv.at[me], row_out, row_in.at[k // GROUP],
             device_id=(ctx, user), device_id_type=MESH,
         ).start()
         return carry
 
-    lax.fori_loop(1, devices, ask, 0)
-    landed[pl.ds(me, 1)] = req[pl.ds(me, 1)]
-    for g in range(groups):
+    def read(g):
+        some = landed.at[pl.ds(g * GROUP, GROUP)]
+        return pltpu.make_async_copy(some, arrived.at[pl.ds(g * GROUP, GROUP)], read_in.at[g])
+
+    def come(g):
         some = req.at[pl.ds(0, GROUP - (1 if g == 0 else 0))]
         pltpu.make_async_copy(some, some, req_in.at[g]).wait()
-    mine = pltpu.make_async_copy(landed, arrived, own_sem)
-    mine.start()
-    mine.wait()
-
-    def gather(asker):
-        for i in range(CAP):
-            gathered[pl.ds(i, 1)] = table[pl.ds(arrived[asker, i], 1)]
-        return gathered[...].astype(BF16)
-
-    def answer(k, carry):
-        ctx, user = moved(k, -1)
-        asker = ctx * lax.axis_size("user") + user
-        send[asker] = gather(asker)
-        pltpu.make_async_remote_copy(
-            send.at[asker], recv.at[me], row_out, row_in.at[k // GROUP],
-            device_id=(ctx, user), device_id_type=MESH,
-        ).start()
-        return carry
+        read(g).start()
+
+    def asks(g):
+        lax.fori_loop(g * GROUP + (1 if g == 0 else 0), (g + 1) * GROUP, ask, 0, unroll=True)
 
     for g in range(groups):
-        first = 1 if g == 0 else 0
-        lax.fori_loop(g * GROUP + first, (g + 1) * GROUP, answer, 0)
-    recv[me] = gather(me)
+        asks(g)
+    come(0)
+    for g in range(groups):
+        if g + 1 < groups:
+            come(g + 1)
+        read(g).wait()
+        lax.fori_loop(g * GROUP + (1 if g == 0 else 0), (g + 1) * GROUP, answer, 0)
+    recv[me] = gather(0)
 
     def unpack(k, carry):
         ctx, user = moved(k, 1)
-        owner = ctx * lax.axis_size("user") + user
+        owner = ctx * users + user
         rows_ref[owner] = recv[owner].astype(F32)
         return carry
 
     for g in range(groups):
-        first = 1 if g == 0 else 0
-        some = recv.at[pl.ds(0, GROUP - first)]
+        some = recv.at[pl.ds(0, GROUP - (1 if g == 0 else 0))]
         pltpu.make_async_copy(some, some, row_in.at[g]).wait()
         lax.fori_loop(g * GROUP, (g + 1) * GROUP, unpack, 0)
     some = req.at[pl.ds(0, devices - 1)]
@@ -151,32 +146,39 @@
     pltpu.make_async_copy(some, some, row_out).wait()
 
 
-def fetch(requests, table):
+def fetch(owner, slot, table):
     devices = lax.axis_size("ctx") * lax.axis_size("user")
+    groups = devices // GROUP
     vmem = pl.BlockSpec(memory_space=pltpu.VMEM)
     return pl.pallas_call(
         fetch_kernel,
-        out_shape=jax.ShapeDtypeStruct((devices, CAP, table.shape[1]), F32),
-        in_specs=[vmem] * 2,
-        out_specs=vmem,
+        out_shape=(
+            jax.ShapeDtypeStruct((devices, CAP, table.shape[1]), F32),
+            jax.ShapeDtypeStruct(owner.shape, jnp.int32),
+        ),
+        in_specs=[vmem, vmem, pl.BlockSpec(memory_space=pl.ANY)],
+        out_specs=(vmem, vmem),
         scratch_shapes=[
             pltpu.VMEM((devices, 128), jnp.int32),
+            pltpu.VMEM((devices, 128), jnp.int32),
             pltpu.SMEM((devices, 128), jnp.int32),
+            pltpu.VMEM(table.shape, BF16),
             pltpu.VMEM(table.shape, F32),
             pltpu.VMEM((CAP, table.shape[1]), F32),
             pltpu.VMEM((devices, CAP, table.shape[1]), BF16),
             pltpu.VMEM((devices, CAP, table.shape[1]), BF16),
             pltpu.SemaphoreType.DMA,
-            pltpu.SemaphoreType.DMA((devices // GROUP,)),
-            pltpu.SemaphoreType.DMA,
-            pltpu.SemaphoreType.DMA,
-            pltpu.SemaphoreType.DMA((devices // GROUP,)),
+            pltpu.SemaphoreType.DMA,
+            pltpu.SemaphoreType.DMA((groups,)),
+            pltpu.SemaphoreType.DMA((groups,)),
+            pltpu.SemaphoreType.DMA,
+            pltpu.SemaphoreType.DMA((groups,)),
         ],
         compiler_params=pltpu.CompilerParams(
             collective_id=0, has_side_effects=True, vmem_limit_bytes=48 << 20
         ),
         name="fetch",
-    )(requests, table)
+    )(owner, slot, table)
 
 
 def attend_kernel(
@@ -344,8 +346,7 @@
 ):
     owner = jnp.swapaxes(block_owner[0], 0, 1)
     slot = jnp.swapaxes(block_slot[0], 0, 1)
-    requests, index = rank(owner, slot)
-    rows = fetch(requests, robe_array)
+    rows, index = fetch(owner, slot, robe_array)
     encoded = attend(
         index, rows.reshape(-1, rows.shape[2]), w_query, w_key, w_value, w_gate, w_output,
         head_gain.reshape(1, -1),

time: 92.9 us -> 90.9 us (0.978)
  Pallas kernels: 89.4 us -> 80.8 us
  local copies, waits for them, and re-layouts: 3.07 us -> 9.51 us
    pallas_call x2 -> x1, Pallas kernels: 66.5 us -> 57.8 us  [fetch(): pl.pallas_call(fetch_kernel, out_shape=(jax.ShapeDtypeStruct((devices, CA...]
    unnamed x19, local copies, waits for them, and re-layouts: 3.07 us -> 9.51 us
where the time goes in v2:
time: 90.9 us; the launch traced here: 90.4 us
  Pallas kernels  80.8 us (89%)
  local copies, waits for them, and re-layouts  9.51 us (10%)
    pallas_call x1, Pallas kernels, fetch(): pl.pallas_call(fetch_kernel, out_shape=(jax.ShapeDtypeStruct((devices, CA...  57.8 us
    pallas_call x1, Pallas kernels, attend(): pl.pallas_call(attend_kernel, out_shape=jax.ShapeDtypeStruct((positions,...  23 us
    unnamed x19, local copies, waits for them, and re-layouts  9.51 us

profile of v2, /device:TPU:1, one launch (start us, length us, event | category | flops | bytes accessed | tf_op | source)
XLA Modules:
  0.0 90.4 jit_solution(7539483063816273649)
XLA Ops:
  0.0 0.0 copy-start
  0.0 1.2 %copy-done = bf16[4096,128]{1,0:T(8,128)(2,1)S(1)} copy-done((bf16[4096,128]{1,0:T(8,128)(2,1)S(1)}, bf16[4096,128]{1,0:T(8,128)(2,1)}, u32[]{:S(2)}) %copy-start) | copy-done | bytes 1048600
  1.2 0.0 copy-start.6
  1.2 0.7 copy-done.6
  1.9 0.0 copy-start.7
  1.9 0.7 copy-done.7
  2.7 57.8 %fetch.1 = (f32[128,80,128]{2,1,0:T(8,128)}, s32[4,1024]{1,0:T(4,128)S(1)}) custom-call(s32[4,1024]{1,0:T(4,128)S(1)} %bitcast.10, s32[4,1024]{1,0:T(4,128)S(1)} %bitcast.11, bf16[4096,128]{1,0:T(8,128)(2,1)S(1)} %copy-done), custom_call_target="tpu_custom_call" | custom-call | tf_op jit(solution)/shard_map/fetch/pallas_call | solution.py:153
  60.5 0.0 copy-start.1
  60.5 1.0 %copy-done.1 = bf16[512,512]{1,0:T(8,128)(2,1)S(1)} copy-done((bf16[512,512]{1,0:T(8,128)(2,1)S(1)}, bf16[512,512]{1,0:T(8,128)(2,1)}, u32[]{:S(2)}) %copy-start.1) | copy-done | bytes 524312
  61.5 0.0 copy-start.2
  61.5 1.0 %copy-done.2 = bf16[512,512]{1,0:T(8,128)(2,1)S(1)} copy-done((bf16[512,512]{1,0:T(8,128)(2,1)S(1)}, bf16[512,512]{1,0:T(8,128)(2,1)}, u32[]{:S(2)}) %copy-start.2) | copy-done | bytes 524312
  62.6 0.0 copy-start.3
  62.6 1.0 %copy-done.3 = bf16[512,512]{1,0:T(8,128)(2,1)S(1)} copy-done((bf16[512,512]{1,0:T(8,128)(2,1)S(1)}, bf16[512,512]{1,0:T(8,128)(2,1)}, u32[]{:S(2)}) %copy-start.3) | copy-done | bytes 524312
  63.6 0.0 copy-start.4
  63.6 1.0 %copy-done.4 = bf16[512,512]{1,0:T(8,128)(2,1)S(1)} copy-done((bf16[512,512]{1,0:T(8,128)(2,1)S(1)}, bf16[512,512]{1,0:T(8,128)(2,1)}, u32[]{:S(2)}) %copy-start.4) | copy-done | bytes 524312
  64.6 0.0 copy-start.5
  64.6 1.0 %copy-done.5 = bf16[512,512]{1,0:T(8,128)(2,1)S(1)} copy-done((bf16[512,512]{1,0:T(8,128)(2,1)S(1)}, bf16[512,512]{1,0:T(8,128)(2,1)}, u32[]{:S(2)}) %copy-start.5) | copy-done | bytes 524312
  65.7 0.0 copy-start.8
  65.7 0.7 copy-done.8
  66.4 23.0 %attend.1 = bf16[1024,512]{1,0:T(8,128)(2,1)S(1)} custom-call(s32[4,1024]{1,0:T(4,128)S(1)} %get-tuple-element.7.index_ref, f32[10240,128]{1,0:T(8,128)} %bitcast.13, bf16[512,512]{1,0:T(8,128)(2,1)S(1)} %copy-done.1, bf16[512,512]{1,0:T(8,128)(2,1)S(1)} %copy-done.2, bf16[512,512]{1,0:T(8,128)(2,1)S(1)} %copy-done.3, bf16[512,512]{1,0:T(8,128)(2,1)S(1)} %copy-done.4, ...), custom_call_target="tpu_custom_call" | custom-call | tf_op jit(solution)/shard_map/attend/pallas_call | solution.py:318
  89.4 1.0 %copy.11 = bf16[1,1024,512]{2,1,0:T(8,128)(2,1)} copy(bf16[1,1024,512]{2,1,0:T(8,128)(2,1)S(1)} %bitcast.9) | data formatting | bytes 2097152
Async XLA Ops:
  0.0 1.2 %copy-start = (bf16[4096,128]{1,0:T(8,128)(2,1)S(1)}, bf16[4096,128]{1,0:T(8,128)(2,1)}, u32[]{:S(2)}) copy-start(bf16[4096,128]{1,0:T(8,128)(2,1)} %table_hbm.1) | copy-start | bytes 3145732
  1.2 0.7 copy-start.6
  1.9 0.7 copy-start.7
  60.5 1.0 %copy-start.1 = (bf16[512,512]{1,0:T(8,128)(2,1)S(1)}, bf16[512,512]{1,0:T(8,128)(2,1)}, u32[]{:S(2)}) copy-start(bf16[512,512]{1,0:T(8,128)(2,1)} %wq_ref.1) | copy-start | bytes 1572868
  61.5 1.0 %copy-start.2 = (bf16[512,512]{1,0:T(8,128)(2,1)S(1)}, bf16[512,512]{1,0:T(8,128)(2,1)}, u32[]{:S(2)}) copy-start(bf16[512,512]{1,0:T(8,128)(2,1)} %wk_ref.1) | copy-start | bytes 1572868
  62.6 1.0 %copy-start.3 = (bf16[512,512]{1,0:T(8,128)(2,1)S(1)}, bf16[512,512]{1,0:T(8,128)(2,1)}, u32[]{:S(2)}) copy-start(bf16[512,512]{1,0:T(8,128)(2,1)} %wv_ref.1) | copy-start | bytes 1572868
  63.6 1.0 %copy-start.4 = (bf16[512,512]{1,0:T(8,128)(2,1)S(1)}, bf16[512,512]{1,0:T(8,128)(2,1)}, u32[]{:S(2)}) copy-start(bf16[512,512]{1,0:T(8,128)(2,1)} %wg_ref.1) | copy-start | bytes 1572868
  64.6 1.0 %copy-start.5 = (bf16[512,512]{1,0:T(8,128)(2,1)S(1)}, bf16[512,512]{1,0:T(8,128)(2,1)}, u32[]{:S(2)}) copy-start(bf16[512,512]{1,0:T(8,128)(2,1)} %wo_ref.1) | copy-start | bytes 1572868
  65.7 0.7 copy-start.8

commit v3 on v2

--- a/solution.py
+++ b/solution.py
@@ -25,10 +25,12 @@
     return z * 8 + x * 2 + (c + core) % 2, u
 
 
-def fetch_kernel(
-    own_ref, slot_ref, table_hbm, rows_ref, index_ref,
-    req, landed, arrived, packed, table, gathered, send, recv,
-    table_in, req_out, req_in, read_in, row_out, row_in,
+def encoder_kernel(
+    own_hbm, slot_hbm, table_hbm, wq_hbm, wk_hbm, wv_hbm, wg_hbm, wo_hbm, gain_hbm, out_ref,
+    own_ref, slot_ref, packed, wq_ref, wk_ref, wv_ref, wg_ref, wo_ref, gain_ref,
+    ranked, index_ref, req, landed, arrived, table, gathered, send, recv, rows_ref,
+    embed, fq, fk, values, gates, intra, state, parcel, from_each, earlier, entering,
+    loaded, index_in, req_out, req_in, read_in, row_out, row_in, out_a, in_a, out_b, in_b,
 ):
     devices = send.shape[0]
     groups = devices // GROUP
@@ -36,8 +38,20 @@
     me = lax.axis_index("ctx") * users + lax.axis_index("user")
     barrier = pltpu.get_barrier_semaphore()
 
-    load = pltpu.make_async_copy(table_hbm, packed, table_in)
-    load.start()
+    loads = [
+        pltpu.make_async_copy(source, target, loaded.at[n])
+        for n, (source, target) in enumerate(
+            (
+                (own_hbm, own_ref), (slot_hbm, slot_ref), (table_hbm, packed),
+                (wk_hbm, wk_ref), (wv_hbm, wv_ref), (wq_hbm, wq_ref), (wg_hbm, wg_ref),
+                (wo_hbm, wo_ref), (gain_hbm, gain_ref),
+            )
+        )
+    ]
+    for load in loads:
+        load.start()
+    loads[0].wait()
+    loads[1].wait()
 
     parts, positions = own_ref.shape
     device_row = lax.broadcasted_iota(jnp.int32, (devices, CHUNK), 0)
@@ -65,7 +79,8 @@
             count = jnp.dot(hot, upper, preferred_element_type=F32) + before
             before = count[:, CHUNK - 1 :]
             rank = jnp.sum(jnp.where(named, count, 0.0), axis=0, keepdims=True).astype(jnp.int32) - 1
-            index_ref[j : j + 1, p : p + CHUNK] = own * CAP + rank
+            spot = jnp.minimum(jnp.maximum(own * CAP + rank, 0), devices * CAP - 1)
+            ranked[j : j + 1, p : p + CHUNK] = spot
             at_rank = rank_row == rank
             high = jnp.where(at_rank, (slot >> 6).astype(F32), 0.0).astype(BF16)
             low = jnp.where(at_rank, (slot & 63).astype(F32), 0.0).astype(BF16)
@@ -76,7 +91,9 @@
     asked = (total[:, :128] * 64.0 + total[:, 128:]).astype(jnp.int32)
     req[...] = jnp.minimum(jnp.maximum(asked, 0), table.shape[0] - 1)
     landed[pl.ds(0, 1)] = req[pl.ds(me, 1)]
-    load.wait()
+    place = pltpu.make_async_copy(ranked, index_ref, index_in)
+    place.start()
+    loads[2].wait()
 
     def widen(k, carry):
         s = pl.ds(pl.multiple_of(k * 256, 256), 256)
@@ -133,73 +150,19 @@
     def unpack(k, carry):
         ctx, user = moved(k, 1)
         owner = ctx * users + user
-        rows_ref[owner] = recv[owner].astype(F32)
+        s = pl.ds(pl.multiple_of(owner * CAP, CAP), CAP)
+        rows_ref[s] = recv[owner].astype(F32)
         return carry
 
     for g in range(groups):
         some = recv.at[pl.ds(0, GROUP - (1 if g == 0 else 0))]
         pltpu.make_async_copy(some, some, row_in.at[g]).wait()
         lax.fori_loop(g * GROUP, (g + 1) * GROUP, unpack, 0)
-    some = req.at[pl.ds(0, devices - 1)]
-    pltpu.make_async_copy(some, some, req_out).wait()
-    some = send.at[pl.ds(0, devices - 1)]
-    pltpu.make_async_copy(some, some, row_out).wait()
-
-
-def fetch(owner, slot, table):
-    devices = lax.axis_size("ctx") * lax.axis_size("user")
-    groups = devices // GROUP
-    vmem = pl.BlockSpec(memory_space=pltpu.VMEM)
-    return pl.pallas_call(
-        fetch_kernel,
-        out_shape=(
-            jax.ShapeDtypeStruct((devices, CAP, table.shape[1]), F32),
-            jax.ShapeDtypeStruct(owner.shape, jnp.int32),
-        ),
-        in_specs=[vmem, vmem, pl.BlockSpec(memory_space=pl.ANY)],
-        out_specs=(vmem, vmem),
-        scratch_shapes=[
-            pltpu.VMEM((devices, 128), jnp.int32),
-            pltpu.VMEM((devices, 128), jnp.int32),
-            pltpu.SMEM((devices, 128), jnp.int32),
-            pltpu.VMEM(table.shape, BF16),
-            pltpu.VMEM(table.shape, F32),
-            pltpu.VMEM((CAP, table.shape[1]), F32),
-            pltpu.VMEM((devices, CAP, table.shape[1]), BF16),
-            pltpu.VMEM((devices, CAP, table.shape[1]), BF16),
-            pltpu.SemaphoreType.DMA,
-            pltpu.SemaphoreType.DMA,
-            pltpu.SemaphoreType.DMA((groups,)),
-            pltpu.SemaphoreType.DMA((groups,)),
-            pltpu.SemaphoreType.DMA,
-            pltpu.SemaphoreType.DMA((groups,)),
-        ],
-        compiler_params=pltpu.CompilerParams(
-            collective_id=0, has_side_effects=True, vmem_limit_bytes=48 << 20
-        ),
-        name="fetch",
-    )(owner, slot, table)
-
-
-def attend_kernel(
-    index_ref, rows_ref, wq_ref, wk_ref, wv_ref, wg_ref, wo_ref, gain_ref, out_ref,
-    embed, fq, fk, values, gates, intra, state, packed, from_each, earlier, entering,
-    out_a, in_a, out_b, in_b,
-):
     ctx_size = lax.axis_size("ctx")
     ctx, user = lax.axis_index("ctx"), lax.axis_index("user")
-    barrier = pltpu.get_barrier_semaphore()
-
-    def greet(k, carry):
-        pl.semaphore_signal(
-            barrier, inc=1, device_id=((ctx + k) % ctx_size, user), device_id_type=MESH
-        )
-        return carry
-
-    lax.fori_loop(1, ctx_size, greet, 0)
-
-    parts, positions = index_ref.shape
     chunks = positions // CHUNK
+
+    place.wait()
 
     def collect(b, carry):
         for i in range(16):
@@ -208,6 +171,9 @@
         return carry
 
     lax.fori_loop(0, positions // 16, collect, 0)
+
+    for load in loads[3:]:
+        load.wait()
 
     def feature(v):
         v = v.astype(BF16).astype(F32)
@@ -230,20 +196,18 @@
     rows = HEADS * HEAD // ctx_size
     for h in range(HEADS):
         for i in range(HEAD // rows):
-            packed[h * (HEAD // rows) + i] = running[h][i * rows : (i + 1) * rows].astype(BF16)
-
-    pl.semaphore_wait(barrier, ctx_size - 1)
+            parcel[h * (HEAD // rows) + i] = running[h][i * rows : (i + 1) * rows].astype(BF16)
 
     def part_out(k, carry):
         other = (ctx + k) % ctx_size
         pltpu.make_async_remote_copy(
-            packed.at[other], from_each.at[ctx], out_a, in_a,
+            parcel.at[other], from_each.at[ctx], out_a, in_a,
             device_id=(other, user), device_id_type=MESH,
         ).start()
         return carry
 
     lax.fori_loop(1, ctx_size, part_out, 0)
-    from_each[ctx] = packed[ctx]
+    from_each[ctx] = parcel[ctx]
 
     causal = lax.broadcasted_iota(jnp.int32, (CHUNK, CHUNK), 0) >= lax.broadcasted_iota(
         jnp.int32, (CHUNK, CHUNK), 1
@@ -266,7 +230,7 @@
     for c in range(chunks // 2):
         local(c)
 
-    some = packed.at[pl.ds(0, ctx_size - 1)]
+    some = parcel.at[pl.ds(0, ctx_size - 1)]
     pltpu.make_async_copy(some, some, in_a).wait()
     pltpu.make_async_copy(some, some, out_a).wait()
     sofar = jnp.zeros((rows, HEAD), F32)
@@ -307,38 +271,53 @@
         out_ref[at] = jnp.dot(
             jnp.concatenate(heads, axis=1), wo_ref[...], preferred_element_type=F32
         ).astype(BF16)
-
-
-def attend(index, rows, wq, wk, wv, wg, wo, gain):
+    some = req.at[pl.ds(0, devices - 1)]
+    pltpu.make_async_copy(some, some, req_out).wait()
+    some = send.at[pl.ds(0, devices - 1)]
+    pltpu.make_async_copy(some, some, row_out).wait()
+
+
+def encoder(owner, slot, table, wq, wk, wv, wg, wo, gain):
     ctx_size = lax.axis_size("ctx")
-    parts, positions = index.shape
+    devices = ctx_size * lax.axis_size("user")
+    groups = devices // GROUP
+    parts, positions = owner.shape
+    block = table.shape[1]
     width = wq.shape[1]
-    vmem = pl.BlockSpec(memory_space=pltpu.VMEM)
+    args = (owner, slot, table, wq, wk, wv, wg, wo, gain)
+    whole = pltpu.VMEM((positions, width), BF16)
     piece = pltpu.VMEM((ctx_size, HEADS * HEAD // ctx_size, HEAD), BF16)
+    one, many = pltpu.SemaphoreType.DMA, pltpu.SemaphoreType.DMA((groups,))
     return pl.pallas_call(
-        attend_kernel,
+        encoder_kernel,
         out_shape=jax.ShapeDtypeStruct((positions, width), BF16),
-        in_specs=[pl.BlockSpec(memory_space=pltpu.SMEM)] + [vmem] * 7,
-        out_specs=vmem,
-        scratch_shapes=[
-            pltpu.VMEM((parts, positions, width // parts), F32),
-            pltpu.VMEM((positions, width), BF16),
-            pltpu.VMEM((positions, width), BF16),
-            pltpu.VMEM((positions, width), BF16),
-            pltpu.VMEM((positions, width), BF16),
+        in_specs=[pl.BlockSpec(memory_space=pltpu.HBM)] * len(args),
+        out_specs=pl.BlockSpec(memory_space=pltpu.VMEM),
+        scratch_shapes=[pltpu.VMEM(a.shape, a.dtype) for a in args]
+        + [
+            pltpu.VMEM((parts, positions), jnp.int32),
+            pltpu.SMEM((parts, positions), jnp.int32),
+            pltpu.VMEM((devices, 128), jnp.int32),
+            pltpu.VMEM((devices, 128), jnp.int32),
+            pltpu.SMEM((devices, 128), jnp.int32),
+            pltpu.VMEM(table.shape, F32),
+            pltpu.VMEM((CAP, block), F32),
+            pltpu.VMEM((devices, CAP, block), BF16),
+            pltpu.VMEM((devices, CAP, block), BF16),
+            pltpu.VMEM((devices * CAP, block), F32),
+            pltpu.VMEM((parts, positions, block), F32),
+            whole, whole, whole, whole,
             pltpu.VMEM((positions, width), F32),
             pltpu.VMEM((positions // CHUNK, HEADS, HEAD, HEAD), F32),
             piece, piece, piece, piece,
-            pltpu.SemaphoreType.DMA,
-            pltpu.SemaphoreType.DMA,
-            pltpu.SemaphoreType.DMA,
-            pltpu.SemaphoreType.DMA,
+            pltpu.SemaphoreType.DMA((len(args),)),
+            one, one, many, many, one, many, one, one, one, one,
         ],
         compiler_params=pltpu.CompilerParams(
-            collective_id=1, has_side_effects=True, vmem_limit_bytes=48 << 20
+            collective_id=0, has_side_effects=True, vmem_limit_bytes=40 << 20
         ),
-        name="attend",
-    )(index, rows, wq, wk, wv, wg, wo, gain)
+        name="encoder",
+    )(*args)
 
 
 def shards(
@@ -346,9 +325,8 @@
 ):
     owner = jnp.swapaxes(block_owner[0], 0, 1)
     slot = jnp.swapaxes(block_slot[0], 0, 1)
-    rows, index = fetch(owner, slot, robe_array)
-    encoded = attend(
-        index, rows.reshape(-1, rows.shape[2]), w_query, w_key, w_value, w_gate, w_output,
+    encoded = encoder(
+        owner, slot, robe_array, w_query, w_key, w_value, w_gate, w_output,
         head_gain.reshape(1, -1),
     )
     return encoded[None]

time: 90.9 us -> 85.9 us (0.945)
  Pallas kernels: 80.8 us -> 75.9 us
    pallas_call x2 -> x1, Pallas kernels: 80.8 us -> 75.9 us  [encoder(): pl.pallas_call(encoder_kernel, out_shape=jax.ShapeDtypeStruct((positions,...]
where the time goes in v3:
time: 85.9 us; the launch traced here: 85.4 us
  Pallas kernels  75.9 us (88%)
  local copies, waits for them, and re-layouts  9.52 us (11%)
    pallas_call x1, Pallas kernels, encoder(): pl.pallas_call(encoder_kernel, out_shape=jax.ShapeDtypeStruct((positions,...  75.9 us
    unnamed x19, local copies, waits for them, and re-layouts  9.52 us

profile of v3, /device:TPU:1, one launch (start us, length us, event | category | flops | bytes accessed | tf_op | source)
XLA Modules:
  0.0 85.4 jit_solution(195906958109391134)
XLA Ops:
  0.0 0.0 copy-start.8
  0.0 0.7 copy-done.8
  0.7 0.0 copy-start
  0.7 1.2 %copy-done = bf16[4096,128]{1,0:T(8,128)(2,1)S(1)} copy-done((bf16[4096,128]{1,0:T(8,128)(2,1)S(1)}, bf16[4096,128]{1,0:T(8,128)(2,1)}, u32[]{:S(2)}) %copy-start) | copy-done | bytes 1048600
  1.9 0.0 copy-start.1
  1.9 1.0 %copy-done.1 = bf16[512,512]{1,0:T(8,128)(2,1)S(1)} copy-done((bf16[512,512]{1,0:T(8,128)(2,1)S(1)}, bf16[512,512]{1,0:T(8,128)(2,1)}, u32[]{:S(2)}) %copy-start.1) | copy-done | bytes 524312
  3.0 0.0 copy-start.2
  3.0 1.0 %copy-done.2 = bf16[512,512]{1,0:T(8,128)(2,1)S(1)} copy-done((bf16[512,512]{1,0:T(8,128)(2,1)S(1)}, bf16[512,512]{1,0:T(8,128)(2,1)}, u32[]{:S(2)}) %copy-start.2) | copy-done | bytes 524312
  4.0 0.0 copy-start.3
  4.0 1.0 %copy-done.3 = bf16[512,512]{1,0:T(8,128)(2,1)S(1)} copy-done((bf16[512,512]{1,0:T(8,128)(2,1)S(1)}, bf16[512,512]{1,0:T(8,128)(2,1)}, u32[]{:S(2)}) %copy-start.3) | copy-done | bytes 524312
  5.0 0.0 copy-start.4
  5.0 1.0 %copy-done.4 = bf16[512,512]{1,0:T(8,128)(2,1)S(1)} copy-done((bf16[512,512]{1,0:T(8,128)(2,1)S(1)}, bf16[512,512]{1,0:T(8,128)(2,1)}, u32[]{:S(2)}) %copy-start.4) | copy-done | bytes 524312
  6.1 0.0 copy-start.5
  6.1 1.0 %copy-done.5 = bf16[512,512]{1,0:T(8,128)(2,1)S(1)} copy-done((bf16[512,512]{1,0:T(8,128)(2,1)S(1)}, bf16[512,512]{1,0:T(8,128)(2,1)}, u32[]{:S(2)}) %copy-start.5) | copy-done | bytes 524312
  7.1 0.0 copy-start.6
  7.1 0.7 copy-done.6
  7.8 0.0 copy-start.7
  7.8 0.7 copy-done.7
  8.6 75.9 %encoder.1 = bf16[1024,512]{1,0:T(8,128)(2,1)S(1)} custom-call(s32[4,1024]{1,0:T(4,128)S(1)} %bitcast.9, s32[4,1024]{1,0:T(4,128)S(1)} %bitcast.10, bf16[4096,128]{1,0:T(8,128)(2,1)S(1)} %copy-done, bf16[512,512]{1,0:T(8,128)(2,1)S(1)} %copy-done.1, bf16[512,512]{1,0:T(8,128)(2,1)S(1)} %copy-done.2, bf16[512,512]{1,0:T(8,128)(2,1)S(1)} %copy-done.3, ...), custom_call_target="tpu_custom_call" | custom-call | tf_op jit(solution)/shard_map/encoder/pallas_call | solution.py:291
  84.4 1.0 %copy.11 = bf16[1,1024,512]{2,1,0:T(8,128)(2,1)} copy(bf16[1,1024,512]{2,1,0:T(8,128)(2,1)S(1)} %bitcast.8) | data formatting | bytes 2097152
Async XLA Ops:
  0.0 0.7 copy-start.8
  0.7 1.2 %copy-start = (bf16[4096,128]{1,0:T(8,128)(2,1)S(1)}, bf16[4096,128]{1,0:T(8,128)(2,1)}, u32[]{:S(2)}) copy-start(bf16[4096,128]{1,0:T(8,128)(2,1)} %table_hbm.1) | copy-start | bytes 3145732
  1.9 1.0 %copy-start.1 = (bf16[512,512]{1,0:T(8,128)(2,1)S(1)}, bf16[512,512]{1,0:T(8,128)(2,1)}, u32[]{:S(2)}) copy-start(bf16[512,512]{1,0:T(8,128)(2,1)} %wq_hbm.1) | copy-start | bytes 1572868
  3.0 1.0 %copy-start.2 = (bf16[512,512]{1,0:T(8,128)(2,1)S(1)}, bf16[512,512]{1,0:T(8,128)(2,1)}, u32[]{:S(2)}) copy-start(bf16[512,512]{1,0:T(8,128)(2,1)} %wk_hbm.1) | copy-start | bytes 1572868
  4.0 1.0 %copy-start.3 = (bf16[512,512]{1,0:T(8,128)(2,1)S(1)}, bf16[512,512]{1,0:T(8,128)(2,1)}, u32[]{:S(2)}) copy-start(bf16[512,512]{1,0:T(8,128)(2,1)} %wv_hbm.1) | copy-start | bytes 1572868
  5.0 1.0 %copy-start.4 = (bf16[512,512]{1,0:T(8,128)(2,1)S(1)}, bf16[512,512]{1,0:T(8,128)(2,1)}, u32[]{:S(2)}) copy-start(bf16[512,512]{1,0:T(8,128)(2,1)} %wg_hbm.1) | copy-start | bytes 1572868
  6.1 1.0 %copy-start.5 = (bf16[512,512]{1,0:T(8,128)(2,1)S(1)}, bf16[512,512]{1,0:T(8,128)(2,1)}, u32[]{:S(2)}) copy-start(bf16[512,512]{1,0:T(8,128)(2,1)} %wo_hbm.1) | copy-start | bytes 1572868
  7.1 0.7 copy-start.6
  7.8 0.7 copy-start.7

commit v4 on v3

--- a/solution.py
+++ b/solution.py
@@ -26,17 +26,25 @@
 
 
 def encoder_kernel(
-    own_hbm, slot_hbm, table_hbm, wq_hbm, wk_hbm, wv_hbm, wg_hbm, wo_hbm, gain_hbm, out_ref,
-    own_ref, slot_ref, packed, wq_ref, wk_ref, wv_ref, wg_ref, wo_ref, gain_ref,
-    ranked, index_ref, req, landed, arrived, table, gathered, send, recv, rows_ref,
-    embed, fq, fk, values, gates, intra, state, parcel, from_each, earlier, entering,
-    loaded, index_in, req_out, req_in, read_in, row_out, row_in, out_a, in_a, out_b, in_b,
+    own_hbm, slot_hbm, table_hbm, wq_hbm, wk_hbm, wv_hbm, wg_hbm, gain_hbm, out_ref,
+    own_ref, slot_ref, packed, wq_ref, wk_ref, wv_ref, wg_ref, gain_ref,
+    ranked, index_ref, req, mid, landed, arrived, table, gathered, send, recv, rows_ref,
+    embed, fq, fk, values, scale, intra, state, parcel, from_each, earlier, entering,
+    loaded, index_in, req_out, mid_in, mid_out, land_in, read_in, row_out, row_in, out_a, in_a, out_b, in_b,
 ):
     devices = send.shape[0]
     groups = devices // GROUP
     users = lax.axis_size("user")
     me = lax.axis_index("ctx") * users + lax.axis_index("user")
+    ctx, user = lax.axis_index("ctx"), lax.axis_index("user")
+    chips, lane_size = req.shape[0], req.shape[1]
+    chip, lane = ctx // 2, ctx % 2 * users + user
+    same_lane = [(((chip + k) % chips) * 2 + ctx % 2, user) for k in range(chips)]
+    lanes = [(lane + k) % lane_size for k in range(lane_size)]
+    same_chip = [(chip * 2 + q // users, q % users) for q in lanes]
     barrier = pltpu.get_barrier_semaphore()
+    for peer in same_lane[1:] + same_chip[1:]:
+        pl.semaphore_signal(barrier, inc=1, device_id=peer, device_id_type=MESH)
 
     loads = [
         pltpu.make_async_copy(source, target, loaded.at[n])
@@ -44,7 +52,7 @@
             (
                 (own_hbm, own_ref), (slot_hbm, slot_ref), (table_hbm, packed),
                 (wk_hbm, wk_ref), (wv_hbm, wv_ref), (wq_hbm, wq_ref), (wg_hbm, wg_ref),
-                (wo_hbm, wo_ref), (gain_hbm, gain_ref),
+                (gain_hbm, gain_ref),
             )
         )
     ]
@@ -62,16 +70,9 @@
         1.0, 0.0,
     ).astype(BF16)
     before = jnp.zeros((devices, 1), F32)
-    greeted, greetings = 0, devices * CHUNK // (parts * positions)
     total = jnp.zeros((devices, 256), F32)
     for j in range(parts):
         for p in range(0, positions, CHUNK):
-            for k in range(greeted, greeted + greetings):
-                if k > 0:
-                    pl.semaphore_signal(
-                        barrier, inc=1, device_id=moved(k, 1), device_id_type=MESH
-                    )
-            greeted += greetings
             own = own_ref[j : j + 1, p : p + CHUNK]
             slot = slot_ref[j : j + 1, p : p + CHUNK]
             named = device_row == own
@@ -89,63 +90,61 @@
                 preferred_element_type=F32,
             )
     asked = (total[:, :128] * 64.0 + total[:, 128:]).astype(jnp.int32)
-    req[...] = jnp.minimum(jnp.maximum(asked, 0), table.shape[0] - 1)
-    landed[pl.ds(0, 1)] = req[pl.ds(me, 1)]
+    asked = jnp.minimum(jnp.maximum(asked, 0), table.shape[0] - 1)
+    req[...] = asked.reshape(req.shape)
+    mid[chip] = req[chip]
     place = pltpu.make_async_copy(ranked, index_ref, index_in)
     place.start()
     loads[2].wait()
 
+    pl.semaphore_wait(barrier, chips + lane_size - 2)
+    for peer in same_lane[1:]:
+        pltpu.make_async_remote_copy(
+            req.at[peer[0] // 2], mid.at[chip], req_out, mid_in,
+            device_id=peer, device_id_type=MESH,
+        ).start()
+
     def widen(k, carry):
         s = pl.ds(pl.multiple_of(k * 256, 256), 256)
         table[s] = packed[s].astype(F32)
         return carry
 
     lax.fori_loop(0, table.shape[0] // 256, widen, 0)
-    pl.semaphore_wait(barrier, devices - 1)
-
-    def ask(k, carry):
-        ctx, user = moved(k, 1)
-        pltpu.make_async_remote_copy(
-            req.at[pl.ds(ctx * users + user, 1)], landed.at[pl.ds(k, 1)], req_out,
-            req_in.at[k // GROUP], device_id=(ctx, user), device_id_type=MESH,
-        ).start()
-        return carry
-
-    def gather(k):
+    some = req.at[pl.ds(0, chips - 1)]
+    pltpu.make_async_copy(some, some, mid_in).wait()
+    for peer, q in zip(same_chip[1:], lanes[1:]):
+        pltpu.make_async_remote_copy(
+            mid.at[:, pl.ds(q, 1)], landed.at[:, pl.ds(lane, 1)], mid_out, land_in,
+            device_id=peer, device_id_type=MESH,
+        ).start()
+    mine = pltpu.make_async_copy(
+        mid.at[:, pl.ds(lane, 1)], landed.at[:, pl.ds(lane, 1)], read_in.at[0]
+    )
+    mine.start()
+    mine.wait()
+    some = mid.at[:, pl.ds(0, lane_size - 1)]
+    pltpu.make_async_copy(some, some, land_in).wait()
+    read = pltpu.make_async_copy(landed, arrived, read_in.at[1])
+    read.start()
+    read.wait()
+
+    def gather(ctx, user):
         for i in range(CAP):
-            gathered[pl.ds(i, 1)] = table[pl.ds(arrived[k, i], 1)]
+            slot = arrived[ctx // 2, ctx % 2 * users + user, i]
+            gathered[pl.ds(i, 1)] = table[pl.ds(slot, 1)]
         return gathered[...].astype(BF16)
 
     def answer(k, carry):
-        ctx, user = moved(k, -1)
-        send[k] = gather(k)
+        asker = moved(k, -1)
+        send[k] = gather(*asker)
         pltpu.make_async_remote_copy(
             send.at[k], recv.at[me], row_out, row_in.at[k // GROUP],
-            device_id=(ctx, user), device_id_type=MESH,
-        ).start()
-        return carry
-
-    def read(g):
-        some = landed.at[pl.ds(g * GROUP, GROUP)]
-        return pltpu.make_async_copy(some, arrived.at[pl.ds(g * GROUP, GROUP)], read_in.at[g])
-
-    def come(g):
-        some = req.at[pl.ds(0, GROUP - (1 if g == 0 else 0))]
-        pltpu.make_async_copy(some, some, req_in.at[g]).wait()
-        read(g).start()
-
-    def asks(g):
-        lax.fori_loop(g * GROUP + (1 if g == 0 else 0), (g + 1) * GROUP, ask, 0, unroll=True)
-
-    for g in range(groups):
-        asks(g)
-    come(0)
-    for g in range(groups):
-        if g + 1 < groups:
-            come(g + 1)
-        read(g).wait()
-        lax.fori_loop(g * GROUP + (1 if g == 0 else 0), (g + 1) * GROUP, answer, 0)
-    recv[me] = gather(0)
+            device_id=asker, device_id_type=MESH,
+        ).start()
+        return carry
+
+    lax.fori_loop(1, devices, answer, 0)
+    recv[me] = gather(ctx, user)
 
     def unpack(k, carry):
         ctx, user = moved(k, 1)
@@ -159,7 +158,6 @@
         pltpu.make_async_copy(some, some, row_in.at[g]).wait()
         lax.fori_loop(g * GROUP, (g + 1) * GROUP, unpack, 0)
     ctx_size = lax.axis_size("ctx")
-    ctx, user = lax.axis_index("ctx"), lax.axis_index("user")
     chunks = positions // CHUNK
 
     place.wait()
@@ -206,7 +204,7 @@
         ).start()
         return carry
 
-    lax.fori_loop(1, ctx_size, part_out, 0)
+    lax.fori_loop(1, ctx_size, part_out, 0, unroll=True)
     from_each[ctx] = parcel[ctx]
 
     causal = lax.broadcasted_iota(jnp.int32, (CHUNK, CHUNK), 0) >= lax.broadcasted_iota(
@@ -218,7 +216,8 @@
         e = jnp.concatenate([embed[j, at] for j in range(parts)], axis=1).astype(BF16)
         q = feature(jnp.dot(e, wq_ref[...], preferred_element_type=F32))
         fq[at] = q
-        gates[at] = jnp.dot(e, wg_ref[...], preferred_element_type=F32).astype(BF16)
+        gate = jnp.dot(e, wg_ref[...], preferred_element_type=F32).astype(BF16).astype(F32)
+        scale[at] = gain_ref[...] * (gate / (1.0 + jnp.exp(-gate)))
         for h in range(HEADS):
             s = slice(h * HEAD, (h + 1) * HEAD)
             scores = lax.dot_general(
@@ -246,7 +245,7 @@
         ).start()
         return carry
 
-    lax.fori_loop(1, ctx_size, part_back, 0)
+    lax.fori_loop(1, ctx_size, part_back, 0, unroll=True)
     entering[ctx] = earlier[ctx]
 
     for c in range(chunks // 2, chunks):
@@ -255,6 +254,7 @@
     pltpu.make_async_copy(some, some, in_b).wait()
     pltpu.make_async_copy(some, some, out_b).wait()
 
+    mean = jnp.full((HEAD, HEAD), 1.0 / HEAD, BF16)
     for c in range(chunks):
         at = pl.ds(c * CHUNK, CHUNK)
         heads = []
@@ -264,27 +264,26 @@
             came = entering[h * n : (h + 1) * n].reshape(HEAD, HEAD).astype(F32)
             within = (state[c, h] + came).astype(BF16)
             mixed = intra[at, s] + jnp.dot(fq[at, s], within, preferred_element_type=F32)
-            square = jnp.mean(mixed * mixed, axis=1, keepdims=True)
-            gate = gates[at, s].astype(F32)
-            normed = mixed * lax.rsqrt(square + 1e-6) * gain_ref[:, s]
-            heads.append((normed * (gate / (1.0 + jnp.exp(-gate)))).astype(BF16))
-        out_ref[at] = jnp.dot(
-            jnp.concatenate(heads, axis=1), wo_ref[...], preferred_element_type=F32
-        ).astype(BF16)
-    some = req.at[pl.ds(0, devices - 1)]
+            square = jnp.dot((mixed * mixed).astype(BF16), mean, preferred_element_type=F32)
+            heads.append((mixed * lax.rsqrt(square + 1e-6) * scale[at, s]).astype(BF16))
+        out_ref[at] = jnp.concatenate(heads, axis=1)
+    some = req.at[pl.ds(0, chips - 1)]
     pltpu.make_async_copy(some, some, req_out).wait()
+    some = mid.at[:, pl.ds(0, lane_size - 1)]
+    pltpu.make_async_copy(some, some, mid_out).wait()
     some = send.at[pl.ds(0, devices - 1)]
     pltpu.make_async_copy(some, some, row_out).wait()
 
 
-def encoder(owner, slot, table, wq, wk, wv, wg, wo, gain):
+def encoder(owner, slot, table, wq, wk, wv, wg, gain):
     ctx_size = lax.axis_size("ctx")
     devices = ctx_size * lax.axis_size("user")
     groups = devices // GROUP
     parts, positions = owner.shape
     block = table.shape[1]
     width = wq.shape[1]
-    args = (owner, slot, table, wq, wk, wv, wg, wo, gain)
+    args = (owner, slot, table, wq, wk, wv, wg, gain)
+    requests = pltpu.VMEM((devices // 8, 8, 128), jnp.int32)
     whole = pltpu.VMEM((positions, width), BF16)
     piece = pltpu.VMEM((ctx_size, HEADS * HEAD // ctx_size, HEAD), BF16)
     one, many = pltpu.SemaphoreType.DMA, pltpu.SemaphoreType.DMA((groups,))
@@ -297,24 +296,24 @@
         + [
             pltpu.VMEM((parts, positions), jnp.int32),
             pltpu.SMEM((parts, positions), jnp.int32),
-            pltpu.VMEM((devices, 128), jnp.int32),
-            pltpu.VMEM((devices, 128), jnp.int32),
-            pltpu.SMEM((devices, 128), jnp.int32),
+            requests, requests, requests,
+            pltpu.SMEM((devices // 8, 8, 128), jnp.int32),
             pltpu.VMEM(table.shape, F32),
             pltpu.VMEM((CAP, block), F32),
             pltpu.VMEM((devices, CAP, block), BF16),
             pltpu.VMEM((devices, CAP, block), BF16),
             pltpu.VMEM((devices * CAP, block), F32),
             pltpu.VMEM((parts, positions, block), F32),
-            whole, whole, whole, whole,
+            whole, whole, whole,
+            pltpu.VMEM((positions, width), F32),
             pltpu.VMEM((positions, width), F32),
             pltpu.VMEM((positions // CHUNK, HEADS, HEAD, HEAD), F32),
             piece, piece, piece, piece,
             pltpu.SemaphoreType.DMA((len(args),)),
-            one, one, many, many, one, many, one, one, one, one,
+            one, one, one, one, one, pltpu.SemaphoreType.DMA((2,)), one, many, one, one, one, one,
         ],
         compiler_params=pltpu.CompilerParams(
-            collective_id=0, has_side_effects=True, vmem_limit_bytes=40 << 20
+            collective_id=0, has_side_effects=True, vmem_limit_bytes=56 << 20
         ),
         name="encoder",
     )(*args)
@@ -325,10 +324,10 @@
 ):
     owner = jnp.swapaxes(block_owner[0], 0, 1)
     slot = jnp.swapaxes(block_slot[0], 0, 1)
-    encoded = encoder(
-        owner, slot, robe_array, w_query, w_key, w_value, w_gate, w_output,
-        head_gain.reshape(1, -1),
+    gated = encoder(
+        owner, slot, robe_array, w_query, w_key, w_value, w_gate, head_gain.reshape(1, -1)
     )
+    encoded = jnp.dot(gated, w_output, preferred_element_type=F32).astype(BF16)
     return encoded[None]
 
 

time: 85.9 us -> 75.5 us (0.88)
  local copies, waits for them, and re-layouts: 9.52 us -> 0.01 us
  Pallas kernels: 75.9 us -> 72.4 us
  matrix products: 0 us -> 2.9 us
    unnamed x19 -> x2, local copies, waits for them, and re-layouts: 9.52 us -> 0.01 us
    pallas_call x1, Pallas kernels: 75.9 us -> 72.4 us  [encoder(): pl.pallas_call(encoder_kernel, out_shape=jax.ShapeDtypeStruct((positions,...]
    dot_general x0 -> x1, matrix products: none -> 2.9 us  [shards(): encoded = jnp.dot(gated, w_output, preferred_element_type=F32).astype(BF16)]
where the time goes in v4:
time: 75.5 us; the launch traced here: 75.4 us
  Pallas kernels  72.4 us (96%)
  matrix products  2.9 us (4%)
    pallas_call x1, Pallas kernels, encoder(): pl.pallas_call(encoder_kernel, out_shape=jax.ShapeDtypeStruct((positions,...  72.4 us
    dot_general x1, matrix products, shards(): encoded = jnp.dot(gated, w_output, preferred_element_type=F32).astype(BF16)  2.9 us

profile of v4, /device:TPU:1, one launch (start us, length us, event | category | flops | bytes accessed | tf_op | source)
XLA Modules:
  0.0 75.4 jit_solution(458504771685578442)
XLA Ops:
  0.0 0.0 copy-start
  0.0 72.4 %encoder.1 = bf16[1024,512]{1,0:T(8,128)(2,1)} custom-call(s32[4,1024]{1,0:T(4,128)} %bitcast.11, s32[4,1024]{1,0:T(4,128)} %bitcast.12, bf16[4096,128]{1,0:T(8,128)(2,1)} %table_hbm.1, bf16[512,512]{1,0:T(8,128)(2,1)} %wq_hbm.1, bf16[512,512]{1,0:T(8,128)(2,1)} %wk_hbm.1, bf16[512,512]{1,0:T(8,128)(2,1)} %wv_hbm.1, bf16[512,512]{1,0:T(8,128)(2,1)} %wg_hbm.1, ...), custom_call_target="tpu_custom_call" | custom-call | tf_op jit(solution)/shard_map/encoder/pallas_call | solution.py:290
  72.5 0.0 copy-done
  72.5 2.9 %fusion = bf16[1,1024,512]{2,1,0:T(8,128)(2,1)} fusion(bf16[1024,512]{1,0:T(8,128)(2,1)} %encoder.1, bf16[512,512]{1,0:T(8,128)(2,1)S(1)} %copy-done), kind=kOutput, calls=%fused_computation.1 | convolution fusion | flops 537395200 | bytes 2621440 | tf_op jit(solution)/shard_map/dot_general | solution.py:330
Async XLA Ops:
  0.0 72.5 %copy-start = (bf16[512,512]{1,0:T(8,128)(2,1)S(1)}, bf16[512,512]{1,0:T(8,128)(2,1)}, u32[]{:S(2)}) copy-start(bf16[512,512]{1,0:T(8,128)(2,1)} %param.16) | copy-start | bytes 1572868

commit v5 on v4

--- a/solution.py
+++ b/solution.py
@@ -28,16 +28,17 @@
 def encoder_kernel(
     own_hbm, slot_hbm, table_hbm, wq_hbm, wk_hbm, wv_hbm, wg_hbm, gain_hbm, out_ref,
     own_ref, slot_ref, packed, wq_ref, wk_ref, wv_ref, wg_ref, gain_ref,
-    ranked, index_ref, req, mid, landed, arrived, table, gathered, send, recv, rows_ref,
+    ranked, index_ref, req, landed, arrived, table, gathered, send, recv, rows_ref,
     embed, fq, fk, values, scale, intra, state, parcel, from_each, earlier, entering,
-    loaded, index_in, req_out, mid_in, mid_out, land_in, read_in, row_out, row_in, out_a, in_a, out_b, in_b,
+    loaded, index_in, all_in, req_out, req_in, read_in, row_out, row_in, out_a, in_a, out_b, in_b,
 ):
     devices = send.shape[0]
     groups = devices // GROUP
     users = lax.axis_size("user")
     me = lax.axis_index("ctx") * users + lax.axis_index("user")
     ctx, user = lax.axis_index("ctx"), lax.axis_index("user")
-    chips, lane_size = req.shape[0], req.shape[1]
+    lane_size = users * 2
+    chips = devices // lane_size
     chip, lane = ctx // 2, ctx % 2 * users + user
     same_lane = [(((chip + k) % chips) * 2 + ctx % 2, user) for k in range(chips)]
     lanes = [(lane + k) % lane_size for k in range(lane_size)]
@@ -73,6 +74,10 @@
     total = jnp.zeros((devices, 256), F32)
     for j in range(parts):
         for p in range(0, positions, CHUNK):
+            if j == parts - 1 and p == 0:
+                pl.semaphore_wait(barrier, chips + lane_size - 2)
+                for peer in same_chip[1:]:
+                    pl.semaphore_signal(all_in, inc=1, device_id=peer, device_id_type=MESH)
             own = own_ref[j : j + 1, p : p + CHUNK]
             slot = slot_ref[j : j + 1, p : p + CHUNK]
             named = device_row == own
@@ -90,19 +95,12 @@
                 preferred_element_type=F32,
             )
     asked = (total[:, :128] * 64.0 + total[:, 128:]).astype(jnp.int32)
-    asked = jnp.minimum(jnp.maximum(asked, 0), table.shape[0] - 1)
-    req[...] = asked.reshape(req.shape)
-    mid[chip] = req[chip]
+    req[...] = jnp.minimum(jnp.maximum(asked, 0), table.shape[0] - 1)
+    landed[pl.ds(0, 1)] = req[pl.ds(me, 1)]
     place = pltpu.make_async_copy(ranked, index_ref, index_in)
     place.start()
+
     loads[2].wait()
-
-    pl.semaphore_wait(barrier, chips + lane_size - 2)
-    for peer in same_lane[1:]:
-        pltpu.make_async_remote_copy(
-            req.at[peer[0] // 2], mid.at[chip], req_out, mid_in,
-            device_id=peer, device_id_type=MESH,
-        ).start()
 
     def widen(k, carry):
         s = pl.ds(pl.multiple_of(k * 256, 256), 256)
@@ -110,41 +108,47 @@
         return carry
 
     lax.fori_loop(0, table.shape[0] // 256, widen, 0)
-    some = req.at[pl.ds(0, chips - 1)]
-    pltpu.make_async_copy(some, some, mid_in).wait()
-    for peer, q in zip(same_chip[1:], lanes[1:]):
+    pl.semaphore_wait(all_in, lane_size - 1)
+
+    def ask(k, carry):
+        ctx, user = moved(k, 1)
         pltpu.make_async_remote_copy(
-            mid.at[:, pl.ds(q, 1)], landed.at[:, pl.ds(lane, 1)], mid_out, land_in,
-            device_id=peer, device_id_type=MESH,
+            req.at[pl.ds(ctx * users + user, 1)], landed.at[pl.ds(k, 1)], req_out,
+            req_in.at[k // GROUP], device_id=(ctx, user), device_id_type=MESH,
         ).start()
-    mine = pltpu.make_async_copy(
-        mid.at[:, pl.ds(lane, 1)], landed.at[:, pl.ds(lane, 1)], read_in.at[0]
-    )
-    mine.start()
-    mine.wait()
-    some = mid.at[:, pl.ds(0, lane_size - 1)]
-    pltpu.make_async_copy(some, some, land_in).wait()
-    read = pltpu.make_async_copy(landed, arrived, read_in.at[1])
-    read.start()
-    read.wait()
-
-    def gather(ctx, user):
+        return carry
+
+    lax.fori_loop(1, devices, ask, 0, unroll=True)
+
+    def read(g):
+        some = landed.at[pl.ds(g * GROUP, GROUP)]
+        return pltpu.make_async_copy(some, arrived.at[pl.ds(g * GROUP, GROUP)], read_in.at[g])
+
+    def come(g):
+        some = req.at[pl.ds(0, GROUP - (1 if g == 0 else 0))]
+        pltpu.make_async_copy(some, some, req_in.at[g]).wait()
+        read(g).start()
+
+    def gather(k):
         for i in range(CAP):
-            slot = arrived[ctx // 2, ctx % 2 * users + user, i]
-            gathered[pl.ds(i, 1)] = table[pl.ds(slot, 1)]
+            gathered[pl.ds(i, 1)] = table[pl.ds(arrived[k, i], 1)]
         return gathered[...].astype(BF16)
 
     def answer(k, carry):
-        asker = moved(k, -1)
-        send[k] = gather(*asker)
+        send[k] = gather(k)
         pltpu.make_async_remote_copy(
             send.at[k], recv.at[me], row_out, row_in.at[k // GROUP],
-            device_id=asker, device_id_type=MESH,
+            device_id=moved(k, -1), device_id_type=MESH,
         ).start()
         return carry
 
-    lax.fori_loop(1, devices, answer, 0)
-    recv[me] = gather(ctx, user)
+    come(0)
+    for g in range(groups):
+        if g + 1 < groups:
+            come(g + 1)
+        read(g).wait()
+        lax.fori_loop(g * GROUP + (1 if g == 0 else 0), (g + 1) * GROUP, answer, 0)
+    recv[me] = gather(0)
 
     def unpack(k, carry):
         ctx, user = moved(k, 1)
@@ -267,10 +271,8 @@
             square = jnp.dot((mixed * mixed).astype(BF16), mean, preferred_element_type=F32)
             heads.append((mixed * lax.rsqrt(square + 1e-6) * scale[at, s]).astype(BF16))
         out_ref[at] = jnp.concatenate(heads, axis=1)
-    some = req.at[pl.ds(0, chips - 1)]
+    some = req.at[pl.ds(0, devices - 1)]
     pltpu.make_async_copy(some, some, req_out).wait()
-    some = mid.at[:, pl.ds(0, lane_size - 1)]
-    pltpu.make_async_copy(some, some, mid_out).wait()
     some = send.at[pl.ds(0, devices - 1)]
     pltpu.make_async_copy(some, some, row_out).wait()
 
@@ -283,7 +285,7 @@
     block = table.shape[1]
     width = wq.shape[1]
     args = (owner, slot, table, wq, wk, wv, wg, gain)
-    requests = pltpu.VMEM((devices // 8, 8, 128), jnp.int32)
+    requests = pltpu.VMEM((devices, 128), jnp.int32)
     whole = pltpu.VMEM((positions, width), BF16)
     piece = pltpu.VMEM((ctx_size, HEADS * HEAD // ctx_size, HEAD), BF16)
     one, many = pltpu.SemaphoreType.DMA, pltpu.SemaphoreType.DMA((groups,))
@@ -296,8 +298,8 @@
         + [
             pltpu.VMEM((parts, positions), jnp.int32),
             pltpu.SMEM((parts, positions), jnp.int32),
-            requests, requests, requests,
-            pltpu.SMEM((devices // 8, 8, 128), jnp.int32),
+            requests, requests,
+            pltpu.SMEM((devices, 128), jnp.int32),
             pltpu.VMEM(table.shape, F32),
             pltpu.VMEM((CAP, block), F32),
             pltpu.VMEM((devices, CAP, block), BF16),
@@ -310,7 +312,7 @@
             pltpu.VMEM((positions // CHUNK, HEADS, HEAD, HEAD), F32),
             piece, piece, piece, piece,
             pltpu.SemaphoreType.DMA((len(args),)),
-            one, one, one, one, one, pltpu.SemaphoreType.DMA((2,)), one, many, one, one, one, one,
+            one, pltpu.SemaphoreType.REGULAR, one, many, many, one, many, one, one, one, one,
         ],
         compiler_params=pltpu.CompilerParams(
             collective_id=0, has_side_effects=True, vmem_limit_bytes=56 << 20

time: 75.5 us -> 74.8 us (level)
  no operation moved by 1% of the time
where the time goes in v5:
time: 74.8 us; the launch traced here: 74.6 us
  Pallas kernels  71.7 us (96%)
  matrix products  2.9 us (4%)
    pallas_call x1, Pallas kernels, encoder(): pl.pallas_call(encoder_kernel, out_shape=jax.ShapeDtypeStruct((positions,...  71.7 us
    dot_general x1, matrix products, shards(): encoded = jnp.dot(gated, w_output, preferred_element_type=F32).astype(BF16)  2.9 us

profile of v5, /device:TPU:1, one launch (start us, length us, event | category | flops | bytes accessed | tf_op | source)
XLA Modules:
  0.0 74.6 jit_solution(12908118490336028616)
XLA Ops:
  0.0 0.0 copy-start
  0.0 71.7 %encoder.1 = bf16[1024,512]{1,0:T(8,128)(2,1)} custom-call(s32[4,1024]{1,0:T(4,128)} %bitcast.11, s32[4,1024]{1,0:T(4,128)} %bitcast.12, bf16[4096,128]{1,0:T(8,128)(2,1)} %table_hbm.1, bf16[512,512]{1,0:T(8,128)(2,1)} %wq_hbm.1, bf16[512,512]{1,0:T(8,128)(2,1)} %wk_hbm.1, bf16[512,512]{1,0:T(8,128)(2,1)} %wv_hbm.1, bf16[512,512]{1,0:T(8,128)(2,1)} %wg_hbm.1, ...), custom_call_target="tpu_custom_call" | custom-call | tf_op jit(solution)/shard_map/encoder/pallas_call | solution.py:292
  71.7 0.0 copy-done
  71.7 2.9 %fusion = bf16[1,1024,512]{2,1,0:T(8,128)(2,1)} fusion(bf16[1024,512]{1,0:T(8,128)(2,1)} %encoder.1, bf16[512,512]{1,0:T(8,128)(2,1)S(1)} %copy-done), kind=kOutput, calls=%fused_computation.1 | convolution fusion | flops 537395200 | bytes 2621440 | tf_op jit(solution)/shard_map/dot_general | solution.py:332
Async XLA Ops:
  0.0 71.7 %copy-start = (bf16[512,512]{1,0:T(8,128)(2,1)S(1)}, bf16[512,512]{1,0:T(8,128)(2,1)}, u32[]{:S(2)}) copy-start(bf16[512,512]{1,0:T(8,128)(2,1)} %param.16) | copy-start | bytes 1572868

commit v6 on v5

--- a/solution.py
+++ b/solution.py
@@ -86,7 +86,9 @@
             before = count[:, CHUNK - 1 :]
             rank = jnp.sum(jnp.where(named, count, 0.0), axis=0, keepdims=True).astype(jnp.int32) - 1
             spot = jnp.minimum(jnp.maximum(own * CAP + rank, 0), devices * CAP - 1)
-            ranked[j : j + 1, p : p + CHUNK] = spot
+            for b in range(CHUNK // 128):
+                row = (j * positions + p) // 128 + b
+                ranked[row : row + 1] = spot[:, b * 128 : (b + 1) * 128]
             at_rank = rank_row == rank
             high = jnp.where(at_rank, (slot >> 6).astype(F32), 0.0).astype(BF16)
             low = jnp.where(at_rank, (slot & 63).astype(F32), 0.0).astype(BF16)
@@ -166,13 +168,16 @@
 
     place.wait()
 
+    blocks = positions // 128
+
     def collect(b, carry):
-        for i in range(16):
+        for i in range(128):
             for j in range(parts):
-                embed[j, pl.ds(b * 16 + i, 1)] = rows_ref[pl.ds(index_ref[j, b * 16 + i], 1)]
-        return carry
-
-    lax.fori_loop(0, positions // 16, collect, 0)
+                row = rows_ref[pl.ds(index_ref[j * blocks + b, i], 1)]
+                embed[j, pl.ds(b * 128 + i, 1)] = row
+        return carry
+
+    lax.fori_loop(0, blocks, collect, 0)
 
     for load in loads[3:]:
         load.wait()
@@ -200,15 +205,17 @@
         for i in range(HEAD // rows):
             parcel[h * (HEAD // rows) + i] = running[h][i * rows : (i + 1) * rows].astype(BF16)
 
-    def part_out(k, carry):
-        other = (ctx + k) % ctx_size
+    ways = [(dz, dx, dc) for dz in range(4) for dx in range(4) for dc in range(2)]
+    ways.sort(key=lambda w: -(min(w[0], 4 - w[0]) + min(w[1], 4 - w[1]) + 0.1 * w[2]))
+    others = [
+        (ctx // 8 + dz) % 4 * 8 + (ctx // 2 + dx) % 4 * 2 + (ctx + dc) % 2
+        for dz, dx, dc in ways[:-1]
+    ]
+    for other in others:
         pltpu.make_async_remote_copy(
             parcel.at[other], from_each.at[ctx], out_a, in_a,
             device_id=(other, user), device_id_type=MESH,
         ).start()
-        return carry
-
-    lax.fori_loop(1, ctx_size, part_out, 0, unroll=True)
     from_each[ctx] = parcel[ctx]
 
     causal = lax.broadcasted_iota(jnp.int32, (CHUNK, CHUNK), 0) >= lax.broadcasted_iota(
@@ -241,15 +248,11 @@
         earlier[i] = sofar.astype(BF16)
         sofar = sofar + from_each[i].astype(F32)
 
-    def part_back(k, carry):
-        other = (ctx + k) % ctx_size
+    for other in others:
         pltpu.make_async_remote_copy(
             earlier.at[other], entering.at[ctx], out_b, in_b,
             device_id=(other, user), device_id_type=MESH,
         ).start()
-        return carry
-
-    lax.fori_loop(1, ctx_size, part_back, 0, unroll=True)
     entering[ctx] = earlier[ctx]
 
     for c in range(chunks // 2, chunks):
@@ -296,8 +299,8 @@
         out_specs=pl.BlockSpec(memory_space=pltpu.VMEM),
         scratch_shapes=[pltpu.VMEM(a.shape, a.dtype) for a in args]
         + [
-            pltpu.VMEM((parts, positions), jnp.int32),
-            pltpu.SMEM((parts, positions), jnp.int32),
+            pltpu.VMEM((parts * positions // 128, 128), jnp.int32),
+            pltpu.SMEM((parts * positions // 128, 128), jnp.int32),
             requests, requests,
             pltpu.SMEM((devices, 128), jnp.int32),
             pltpu.VMEM(table.shape, F32),

time: 74.8 us -> 71.8 us (0.960)
  Pallas kernels: 71.7 us -> 68.8 us
    pallas_call x1, Pallas kernels: 71.7 us -> 68.8 us  [encoder(): pl.pallas_call(encoder_kernel, out_shape=jax.ShapeDtypeStruct((positions,...]
where the time goes in v6:
time: 71.8 us; the launch traced here: 71.7 us
  Pallas kernels  68.8 us (96%)
  matrix products  2.9 us (4%)
    pallas_call x1, Pallas kernels, encoder(): pl.pallas_call(encoder_kernel, out_shape=jax.ShapeDtypeStruct((positions,...  68.8 us
    dot_general x1, matrix products, shards(): encoded = jnp.dot(gated, w_output, preferred_element_type=F32).astype(BF16)  2.9 us

profile of v6, /device:TPU:1, one launch (start us, length us, event | category | flops | bytes accessed | tf_op | source)
XLA Modules:
  0.0 71.7 jit_solution(10320653131697525423)
XLA Ops:
  0.0 0.0 copy-start
  0.0 68.8 %encoder.1 = bf16[1024,512]{1,0:T(8,128)(2,1)} custom-call(s32[4,1024]{1,0:T(4,128)} %bitcast.11, s32[4,1024]{1,0:T(4,128)} %bitcast.12, bf16[4096,128]{1,0:T(8,128)(2,1)} %table_hbm.1, bf16[512,512]{1,0:T(8,128)(2,1)} %wq_hbm.1, bf16[512,512]{1,0:T(8,128)(2,1)} %wk_hbm.1, bf16[512,512]{1,0:T(8,128)(2,1)} %wv_hbm.1, bf16[512,512]{1,0:T(8,128)(2,1)} %wg_hbm.1, ...), custom_call_target="tpu_custom_call" | custom-call | tf_op jit(solution)/shard_map/encoder/pallas_call | solution.py:295
  68.8 0.0 copy-done
  68.8 2.9 %fusion = bf16[1,1024,512]{2,1,0:T(8,128)(2,1)} fusion(bf16[1024,512]{1,0:T(8,128)(2,1)} %encoder.1, bf16[512,512]{1,0:T(8,128)(2,1)S(1)} %copy-done), kind=kOutput, calls=%fused_computation.1 | convolution fusion | flops 537395200 | bytes 2621440 | tf_op jit(solution)/shard_map/dot_general | solution.py:335
Async XLA Ops:
  0.0 68.8 %copy-start = (bf16[512,512]{1,0:T(8,128)(2,1)S(1)}, bf16[512,512]{1,0:T(8,128)(2,1)}, u32[]{:S(2)}) copy-start(bf16[512,512]{1,0:T(8,128)(2,1)} %param.16) | copy-start | bytes 1572868

commit v7 on v6

--- a/solution.py
+++ b/solution.py
@@ -11,6 +11,7 @@
 CAP = 80
 GROUP = 16
 CHUNK = 256
+WIDE = 512
 F32 = jnp.float32
 BF16 = jnp.bfloat16
 
@@ -26,11 +27,11 @@
 
 
 def encoder_kernel(
-    own_hbm, slot_hbm, table_hbm, wq_hbm, wk_hbm, wv_hbm, wg_hbm, gain_hbm, out_ref,
+    own_hbm, slot_hbm, table_hbm, wq_hbm, wk_hbm, wv_hbm, wg_hbm, gain_hbm, out_hbm,
     own_ref, slot_ref, packed, wq_ref, wk_ref, wv_ref, wg_ref, gain_ref,
     ranked, index_ref, req, landed, arrived, table, gathered, send, recv, rows_ref,
-    embed, fq, fk, values, scale, intra, state, parcel, from_each, earlier, entering,
-    loaded, index_in, all_in, req_out, req_in, read_in, row_out, row_in, out_a, in_a, out_b, in_b,
+    embed, items, gated, fq, fk, values, scale, intra, state, parcel, from_each, earlier, entering,
+    loaded, stored, index_in, all_in, req_out, req_in, read_in, row_out, row_in, out_a, in_a, out_b, in_b,
 ):
     devices = send.shape[0]
     groups = devices // GROUP
@@ -187,19 +188,22 @@
         return jnp.where(v > 0, v + 1.0, jnp.exp(jnp.minimum(v, 0.0))).astype(BF16)
 
     running = [jnp.zeros((HEAD, HEAD), F32)] * HEADS
-    for c in range(chunks):
-        at = pl.ds(c * CHUNK, CHUNK)
+    for w in range(positions // WIDE):
+        at = pl.ds(w * WIDE, WIDE)
         e = jnp.concatenate([embed[j, at] for j in range(parts)], axis=1).astype(BF16)
+        items[at] = e
         k = feature(jnp.dot(e, wk_ref[...], preferred_element_type=F32))
         v = jnp.dot(e, wv_ref[...], preferred_element_type=F32).astype(BF16)
         fk[at] = k
         values[at] = v
-        for h in range(HEADS):
-            s = slice(h * HEAD, (h + 1) * HEAD)
-            state[c, h] = running[h]
-            running[h] = running[h] + lax.dot_general(
-                k[:, s], v[:, s], (((0,), (0,)), ((), ())), preferred_element_type=F32
-            )
+        for n in range(WIDE // CHUNK):
+            r = slice(n * CHUNK, (n + 1) * CHUNK)
+            for h in range(HEADS):
+                s = slice(h * HEAD, (h + 1) * HEAD)
+                state[w * (WIDE // CHUNK) + n, h] = running[h]
+                running[h] = running[h] + lax.dot_general(
+                    k[r, s], v[r, s], (((0,), (0,)), ((), ())), preferred_element_type=F32
+                )
     rows = HEADS * HEAD // ctx_size
     for h in range(HEADS):
         for i in range(HEAD // rows):
@@ -222,23 +226,26 @@
         jnp.int32, (CHUNK, CHUNK), 1
     )
 
-    def local(c):
-        at = pl.ds(c * CHUNK, CHUNK)
-        e = jnp.concatenate([embed[j, at] for j in range(parts)], axis=1).astype(BF16)
+    def local(w):
+        whole = pl.ds(w * WIDE, WIDE)
+        e = items[whole]
         q = feature(jnp.dot(e, wq_ref[...], preferred_element_type=F32))
-        fq[at] = q
+        fq[whole] = q
         gate = jnp.dot(e, wg_ref[...], preferred_element_type=F32).astype(BF16).astype(F32)
-        scale[at] = gain_ref[...] * (gate / (1.0 + jnp.exp(-gate)))
-        for h in range(HEADS):
-            s = slice(h * HEAD, (h + 1) * HEAD)
-            scores = lax.dot_general(
-                q[:, s], fk[at, s], (((1,), (1,)), ((), ())), preferred_element_type=F32
-            )
-            scores = jnp.where(causal, scores, 0.0).astype(BF16)
-            intra[at, s] = jnp.dot(scores, values[at, s], preferred_element_type=F32)
-
-    for c in range(chunks // 2):
-        local(c)
+        scale[whole] = gain_ref[...] * (gate / (1.0 + jnp.exp(-gate)))
+        for n in range(WIDE // CHUNK):
+            at = pl.ds(w * WIDE + n * CHUNK, CHUNK)
+            for h in range(HEADS):
+                s = slice(h * HEAD, (h + 1) * HEAD)
+                scores = lax.dot_general(
+                    q[n * CHUNK : (n + 1) * CHUNK, s], fk[at, s], (((1,), (1,)), ((), ())),
+                    preferred_element_type=F32,
+                )
+                scores = jnp.where(causal, scores, 0.0).astype(BF16)
+                intra[at, s] = jnp.dot(scores, values[at, s], preferred_element_type=F32)
+
+    for w in range(positions // WIDE // 2):
+        local(w)
 
     some = parcel.at[pl.ds(0, ctx_size - 1)]
     pltpu.make_async_copy(some, some, in_a).wait()
@@ -255,12 +262,13 @@
         ).start()
     entering[ctx] = earlier[ctx]
 
-    for c in range(chunks // 2, chunks):
-        local(c)
+    for w in range(positions // WIDE // 2, positions // WIDE):
+        local(w)
 
     pltpu.make_async_copy(some, some, in_b).wait()
     pltpu.make_async_copy(some, some, out_b).wait()
 
+    stores = []
     mean = jnp.full((HEAD, HEAD), 1.0 / HEAD, BF16)
     for c in range(chunks):
         at = pl.ds(c * CHUNK, CHUNK)
@@ -273,7 +281,11 @@
             mixed = intra[at, s] + jnp.dot(fq[at, s], within, preferred_element_type=F32)
             square = jnp.dot((mixed * mixed).astype(BF16), mean, preferred_element_type=F32)
             heads.append((mixed * lax.rsqrt(square + 1e-6) * scale[at, s]).astype(BF16))
-        out_ref[at] = jnp.concatenate(heads, axis=1)
+        gated[at] = jnp.concatenate(heads, axis=1)
+        stores.append(pltpu.make_async_copy(gated.at[at], out_hbm.at[at], stored.at[c]))
+        stores[c].start()
+    for store in stores:
+        store.wait()
     some = req.at[pl.ds(0, devices - 1)]
     pltpu.make_async_copy(some, some, req_out).wait()
     some = send.at[pl.ds(0, devices - 1)]
@@ -296,7 +308,7 @@
         encoder_kernel,
         out_shape=jax.ShapeDtypeStruct((positions, width), BF16),
         in_specs=[pl.BlockSpec(memory_space=pltpu.HBM)] * len(args),
-        out_specs=pl.BlockSpec(memory_space=pltpu.VMEM),
+        out_specs=pl.BlockSpec(memory_space=pltpu.HBM),
         scratch_shapes=[pltpu.VMEM(a.shape, a.dtype) for a in args]
         + [
             pltpu.VMEM((parts * positions // 128, 128), jnp.int32),
@@ -309,12 +321,13 @@
             pltpu.VMEM((devices, CAP, block), BF16),
             pltpu.VMEM((devices * CAP, block), F32),
             pltpu.VMEM((parts, positions, block), F32),
-            whole, whole, whole,
+            whole, whole, whole, whole, whole,
             pltpu.VMEM((positions, width), F32),
             pltpu.VMEM((positions, width), F32),
             pltpu.VMEM((positions // CHUNK, HEADS, HEAD, HEAD), F32),
             piece, piece, piece, piece,
             pltpu.SemaphoreType.DMA((len(args),)),
+            pltpu.SemaphoreType.DMA((positions // CHUNK,)),
             one, pltpu.SemaphoreType.REGULAR, one, many, many, one, many, one, one, one, one,
         ],
         compiler_params=pltpu.CompilerParams(

time: 71.8 us -> 71.2 us (level)
  no operation moved by 1% of the time
where the time goes in v7:
time: 71.2 us; the launch traced here: 71.1 us
  Pallas kernels  68.2 us (96%)
  matrix products  2.9 us (4%)
    pallas_call x1, Pallas kernels, encoder(): pl.pallas_call(encoder_kernel, out_shape=jax.ShapeDtypeStruct((positions,...  68.2 us
    dot_general x1, matrix products, shards(): encoded = jnp.dot(gated, w_output, preferred_element_type=F32).astype(BF16)  2.9 us

profile of v7, /device:TPU:1, one launch (start us, length us, event | category | flops | bytes accessed | tf_op | source)
XLA Modules:
  0.0 71.1 jit_solution(9147650472345464930)
XLA Ops:
  0.0 0.0 copy-start
  0.0 68.2 %encoder.1 = bf16[1024,512]{1,0:T(8,128)(2,1)} custom-call(s32[4,1024]{1,0:T(4,128)} %bitcast.11, s32[4,1024]{1,0:T(4,128)} %bitcast.12, bf16[4096,128]{1,0:T(8,128)(2,1)} %table_hbm.1, bf16[512,512]{1,0:T(8,128)(2,1)} %wq_hbm.1, bf16[512,512]{1,0:T(8,128)(2,1)} %wk_hbm.1, bf16[512,512]{1,0:T(8,128)(2,1)} %wv_hbm.1, bf16[512,512]{1,0:T(8,128)(2,1)} %wg_hbm.1, ...), custom_call_target="tpu_custom_call" | custom-call | tf_op jit(solution)/shard_map/encoder/pallas_call | solution.py:307
  68.2 0.0 copy-done
  68.2 2.9 %fusion = bf16[1,1024,512]{2,1,0:T(8,128)(2,1)} fusion(bf16[1024,512]{1,0:T(8,128)(2,1)} %encoder.1, bf16[512,512]{1,0:T(8,128)(2,1)S(1)} %copy-done), kind=kOutput, calls=%fused_computation.1 | convolution fusion | flops 537395200 | bytes 2621440 | tf_op jit(solution)/shard_map/dot_general | solution.py:348
Async XLA Ops:
  0.0 68.2 %copy-start = (bf16[512,512]{1,0:T(8,128)(2,1)S(1)}, bf16[512,512]{1,0:T(8,128)(2,1)}, u32[]{:S(2)}) copy-start(bf16[512,512]{1,0:T(8,128)(2,1)} %param.16) | copy-start | bytes 1572868

commit v8 on v7

--- a/solution.py
+++ b/solution.py
@@ -249,7 +249,6 @@
 
     some = parcel.at[pl.ds(0, ctx_size - 1)]
     pltpu.make_async_copy(some, some, in_a).wait()
-    pltpu.make_async_copy(some, some, out_a).wait()
     sofar = jnp.zeros((rows, HEAD), F32)
     for i in range(ctx_size):
         earlier[i] = sofar.astype(BF16)
@@ -266,7 +265,6 @@
         local(w)
 
     pltpu.make_async_copy(some, some, in_b).wait()
-    pltpu.make_async_copy(some, some, out_b).wait()
 
     stores = []
     mean = jnp.full((HEAD, HEAD), 1.0 / HEAD, BF16)
@@ -286,6 +284,9 @@
         stores[c].start()
     for store in stores:
         store.wait()
+    some = parcel.at[pl.ds(0, ctx_size - 1)]
+    pltpu.make_async_copy(some, some, out_a).wait()
+    pltpu.make_async_copy(some, some, out_b).wait()
     some = req.at[pl.ds(0, devices - 1)]
     pltpu.make_async_copy(some, some, req_out).wait()
     some = send.at[pl.ds(0, devices - 1)]

time: 71.2 us -> 71.2 us (level)
  no operation moved by 1% of the time
where the time goes in v8:
time: 71.2 us; the launch traced here: 71.1 us
  Pallas kernels  68.2 us (96%)
  matrix products  2.9 us (4%)
    pallas_call x1, Pallas kernels, encoder(): pl.pallas_call(encoder_kernel, out_shape=jax.ShapeDtypeStruct((positions,...  68.2 us
    dot_general x1, matrix products, shards(): encoded = jnp.dot(gated, w_output, preferred_element_type=F32).astype(BF16)  2.9 us

profile of v8, /device:TPU:1, one launch (start us, length us, event | category | flops | bytes accessed | tf_op | source)
XLA Modules:
  0.0 71.1 jit_solution(2896244035309045757)
XLA Ops:
  0.0 0.0 copy-start
  0.0 68.2 %encoder.1 = bf16[1024,512]{1,0:T(8,128)(2,1)} custom-call(s32[4,1024]{1,0:T(4,128)} %bitcast.11, s32[4,1024]{1,0:T(4,128)} %bitcast.12, bf16[4096,128]{1,0:T(8,128)(2,1)} %table_hbm.1, bf16[512,512]{1,0:T(8,128)(2,1)} %wq_hbm.1, bf16[512,512]{1,0:T(8,128)(2,1)} %wk_hbm.1, bf16[512,512]{1,0:T(8,128)(2,1)} %wv_hbm.1, bf16[512,512]{1,0:T(8,128)(2,1)} %wg_hbm.1, ...), custom_call_target="tpu_custom_call" | custom-call | tf_op jit(solution)/shard_map/encoder/pallas_call | solution.py:308
  68.2 0.0 copy-done
  68.2 2.9 %fusion = bf16[1,1024,512]{2,1,0:T(8,128)(2,1)} fusion(bf16[1024,512]{1,0:T(8,128)(2,1)} %encoder.1, bf16[512,512]{1,0:T(8,128)(2,1)S(1)} %copy-done), kind=kOutput, calls=%fused_computation.1 | convolution fusion | flops 537395200 | bytes 2621440 | tf_op jit(solution)/shard_map/dot_general | solution.py:349
Async XLA Ops:
  0.0 68.2 %copy-start = (bf16[512,512]{1,0:T(8,128)(2,1)S(1)}, bf16[512,512]{1,0:T(8,128)(2,1)}, u32[]{:S(2)}) copy-start(bf16[512,512]{1,0:T(8,128)(2,1)} %param.16) | copy-start | bytes 1572868

commit v9 on v8

--- a/solution.py
+++ b/solution.py
@@ -75,7 +75,7 @@
     total = jnp.zeros((devices, 256), F32)
     for j in range(parts):
         for p in range(0, positions, CHUNK):
-            if j == parts - 1 and p == 0:
+            if j == parts // 2 and p == 0:
                 pl.semaphore_wait(barrier, chips + lane_size - 2)
                 for peer in same_chip[1:]:
                     pl.semaphore_signal(all_in, inc=1, device_id=peer, device_id_type=MESH)

time: 71.2 us -> 71.2 us (level)
  no operation moved by 1% of the time
where the time goes in v9:
time: 71.2 us; the launch traced here: 71 us
  Pallas kernels  68.1 us (96%)
  matrix products  2.9 us (4%)
    pallas_call x1, Pallas kernels, encoder(): pl.pallas_call(encoder_kernel, out_shape=jax.ShapeDtypeStruct((positions,...  68.1 us
    dot_general x1, matrix products, shards(): encoded = jnp.dot(gated, w_output, preferred_element_type=F32).astype(BF16)  2.9 us

profile of v9, /device:TPU:1, one launch (start us, length us, event | category | flops | bytes accessed | tf_op | source)
XLA Modules:
  0.0 71.0 jit_solution(16960215284347256114)
XLA Ops:
  0.0 0.0 copy-start
  0.0 68.1 %encoder.1 = bf16[1024,512]{1,0:T(8,128)(2,1)} custom-call(s32[4,1024]{1,0:T(4,128)} %bitcast.11, s32[4,1024]{1,0:T(4,128)} %bitcast.12, bf16[4096,128]{1,0:T(8,128)(2,1)} %table_hbm.1, bf16[512,512]{1,0:T(8,128)(2,1)} %wq_hbm.1, bf16[512,512]{1,0:T(8,128)(2,1)} %wk_hbm.1, bf16[512,512]{1,0:T(8,128)(2,1)} %wv_hbm.1, bf16[512,512]{1,0:T(8,128)(2,1)} %wg_hbm.1, ...), custom_call_target="tpu_custom_call" | custom-call | tf_op jit(solution)/shard_map/encoder/pallas_call | solution.py:308
  68.1 0.0 copy-done
  68.1 2.9 %fusion = bf16[1,1024,512]{2,1,0:T(8,128)(2,1)} fusion(bf16[1024,512]{1,0:T(8,128)(2,1)} %encoder.1, bf16[512,512]{1,0:T(8,128)(2,1)S(1)} %copy-done), kind=kOutput, calls=%fused_computation.1 | convolution fusion | flops 537395200 | bytes 2621440 | tf_op jit(solution)/shard_map/dot_general | solution.py:349
Async XLA Ops:
  0.0 68.1 %copy-start = (bf16[512,512]{1,0:T(8,128)(2,1)S(1)}, bf16[512,512]{1,0:T(8,128)(2,1)}, u32[]{:S(2)}) copy-start(bf16[512,512]{1,0:T(8,128)(2,1)} %param.16) | copy-start | bytes 1572868
